TPU v7x, 32 devices: a whole 2x2x4 slice. The times are simulated.
32 devices in a mesh: seq: 4 (over z), hid: 8 (over y, x, core).
Axes of the slice: x: 2, y: 2, z: 4, core: 2. Of those that a mesh axis runs over, the one named last changes fastest.
Arguments:
- tokens: bfloat16 [2048, 4, 2048], P(('seq', 'hid')), may hold values from -6 to 6
- lengths: int32 [4], replicated, may hold values from 512 to 2048, as said below
- cotangent: bfloat16 [2048, 4, 2048], P(('seq', 'hid')), may hold values from -6 to 6
- mixer_gain: float32 [2048], replicated, may hold values from 0.25 to 1.75
- query_weight: bfloat16 [2048, 2048], P(None, 'hid'), may hold values from -0.125 to 0.125
- forget_weight: bfloat16 [2048, 2048], P(None, 'hid'), may hold values from -0.125 to 0.125
- input_weight: bfloat16 [2048, 2048], P(None, 'hid'), may hold values from -0.125 to 0.125
- gate_weight: bfloat16 [2048, 2048], P(None, 'hid'), may hold values from -0.125 to 0.125
- lower_bound: float32 [2048], P('hid'), may hold values from 0.5 to 0.9995
- head_gain: float32 [2048], P('hid'), may hold values from 0.25 to 1.75
- out_weight: bfloat16 [2048, 2048], replicated, may hold values from -0.125 to 0.125
- feed_gain: float32 [2048], replicated, may hold values from 0.25 to 1.75
- feed_gate_weight: bfloat16 [2048, 5632], P(None, 'hid'), may hold values from -0.125 to 0.125
- up_weight: bfloat16 [2048, 5632], P(None, 'hid'), may hold values from -0.125 to 0.125
- down_weight: bfloat16 [5632, 2048], P('hid'), may hold values from -0.078125 to 0.078125
Outputs:
- output: bfloat16 [2048, 4, 2048], P(('seq', 'hid'))
- grad_tokens: float32 [2048, 4, 2048], P(('seq', 'hid'))
- grad_mixer_gain: float32 [2048], replicated
- grad_query_weight: float32 [2048, 2048], P(None, 'hid')
- grad_forget_weight: float32 [2048, 2048], P(None, 'hid')
- grad_input_weight: float32 [2048, 2048], P(None, 'hid')
- grad_gate_weight: float32 [2048, 2048], P(None, 'hid')
- grad_lower_bound: float32 [2048], P('hid')
- grad_head_gain: float32 [2048], P('hid')
- grad_out_weight: float32 [2048, 2048], replicated
- grad_feed_gain: float32 [2048], replicated
- grad_feed_gate_weight: float32 [2048, 5632], P(None, 'hid')
- grad_up_weight: float32 [2048, 5632], P(None, 'hid')
- grad_down_weight: float32 [5632, 2048], P('hid')
- mean_forget: float32 [], replicated
Inputs may be any that keep to these rules, and one draw needn't show every extreme that they name: `lengths`: positions at or beyond a sequence's length are padding. One sequence has length exactly 2048 and another exactly 512.
All inputs are finite; a program needn't handle non-finite values.
Results may differ from a plain program's by a relative error of at most 0.009.
The roundings to bfloat16 on the way count: a program that leaves them out, or rounds other values in their place, can miss the bound.
Values may be sent and summed in bfloat16 or wider, within the bound.
No kernel may reach another device: no remote copies, remote signals or barrier semaphores. Data moves between devices by JAX's collectives and lax.ppermute only.
A program may use at most 320 MiB of HBM per device.

v0:
```python
import math

import jax
import jax.numpy as jnp
from jax import lax
from jax.sharding import PartitionSpec as P

HDIM = 128


precise = lax.Precision.HIGHEST


def entering(part, axis, combine, identity, reverse):
    count = lax.axis_size(axis)
    place = lax.axis_index(axis)
    ahead = count - 1 - place if reverse else place
    gathered = jax.tree.map(lambda a: lax.all_gather(a, axis), part)
    state = jax.tree.map(lambda a, e: jnp.zeros_like(a) + jnp.asarray(e, a.dtype), part, identity)

    def one(step, state):
        source = count - 1 - step if reverse else step
        return combine(
            state, jax.tree.map(lambda a: lax.dynamic_index_in_dim(a, source, 0, False), gathered)
        )

    return lax.fori_loop(0, ahead, one, state)


def rms_scale(values, scale_gain, epsilon):
    return (
        values * lax.rsqrt(jnp.mean(values * values, axis=-1, keepdims=True) + epsilon) * scale_gain
    )


def combine_states(earlier, later):
    return (earlier[0] * later[0], later[0][..., None] * earlier[1] + later[1])


def prepare(queries, key_rates, values):
    block_len = queries.shape[1]
    log_keep = jnp.log1p(-key_rates)
    cumulative = jnp.cumsum(log_keep, axis=1)
    middle = cumulative[:, block_len // 2 - 1 : block_len // 2]
    final_cum = cumulative[:, block_len - 1 :]
    query_mid = queries * jnp.exp(cumulative - middle)
    key_mid = key_rates * jnp.exp(middle - cumulative)
    causal = (jnp.arange(block_len)[:, None] >= jnp.arange(block_len)[None, :]).astype(jnp.float32)
    scores = jnp.einsum("btshk,bushk->bshtu", query_mid, key_mid, precision=precise) * causal
    within = jnp.einsum("bshtu,bushv->btshv", scores, values, precision=precise)
    key_to_end = key_rates * jnp.exp(final_cum - cumulative)
    growth = jnp.einsum("bushk,bushv->bshkv", key_to_end, values, precision=precise)
    fading = jnp.exp(final_cum[:, 0])
    return (cumulative, within, growth, fading)


def advance(initial, fading, growth):

    def advance_one(carried, members):
        return (members[0][..., None] * carried + members[1], carried)

    return lax.scan(advance_one, initial, (fading, growth))


def recurrence(queries, key_rates, values, initial):
    cumulative, within, growth, fading = prepare(queries, key_rates, values)
    final_state, starts = advance(initial, fading, growth)
    across = jnp.einsum(
        "btshk,bshkv->btshv", queries * jnp.exp(cumulative), starts, precision=precise
    )
    return (within + across, final_state)


def shards(
    tokens,
    lengths,
    cotangent,
    mixer_gain,
    query_weight,
    forget_weight,
    input_weight,
    gate_weight,
    lower_bound,
    head_gain,
    out_weight,
    feed_gain,
    feed_gate_weight,
    up_weight,
    down_weight,
):
    hid_count = lax.axis_size("hid")
    seq_place = lax.axis_index("seq")
    tok_rows, seq_count, model_width = tokens.shape
    span_len = tok_rows * hid_count
    local_cols = query_weight.shape[1]
    heads_here = local_cols // HDIM
    block_len = math.gcd(64, span_len)
    span_pos = seq_place * span_len + jnp.arange(span_len)
    live_mask = (span_pos[:, None] < lengths[None, :]).astype(jnp.float32)[..., None]
    input_values = tokens.astype(jnp.float32)
    normed_in = rms_scale(input_values, mixer_gain, 1e-06).astype(jnp.bfloat16)
    gathered_in = lax.all_gather(normed_in, "hid", axis=0, tiled=True)
    joint_weight = jnp.concatenate([query_weight, forget_weight, input_weight, gate_weight], axis=1)
    joint_proj = jnp.einsum(
        "psd,de->pse", gathered_in, joint_weight, preferred_element_type=jnp.float32
    )
    queries, forget_pre, values, out_gate = jnp.split(joint_proj, 4, axis=2)

    def rate_of(pre_values, bound):
        return live_mask * (1.0 - bound) * jax.nn.sigmoid(-pre_values)

    key_rates = rate_of(forget_pre, lower_bound)
    forget_total = jnp.sum(live_mask * (1.0 - key_rates))

    def to_blocks(array):
        return array.reshape(span_len // block_len, block_len, seq_count, heads_here, HDIM)

    blocked = (to_blocks(queries), to_blocks(key_rates), to_blocks(values))
    cumulative, within, growth, fading = prepare(*blocked)
    zero_state = jnp.zeros((seq_count, heads_here, HDIM, HDIM), jnp.float32)
    local_end, _ = advance(zero_state, fading, growth)
    device_fade = jnp.exp(jnp.sum(cumulative[:, block_len - 1], axis=0))
    unity = jnp.ones_like(device_fade)
    _, incoming = entering(
        (device_fade, local_end), "seq", combine_states, (unity, zero_state), False
    )
    _, starts = advance(incoming, fading, growth)
    across = jnp.einsum(
        "btshk,bshkv->btshv", blocked[0] * jnp.exp(cumulative), starts, precision=precise
    )
    mixture = (within + across).reshape(span_len, seq_count, heads_here, HDIM)

    def head_finish(mix_values, gate_values, gain_values):
        scaled = mix_values * lax.rsqrt(
            jnp.mean(mix_values * mix_values, axis=-1, keepdims=True) + 1e-05
        )
        return (
            scaled.reshape(gate_values.shape) * gain_values * jax.nn.silu(gate_values) * live_mask
        )

    gated_out = head_finish(mixture, out_gate, head_gain).astype(jnp.bfloat16)
    moved = lax.all_to_all(gated_out, "hid", split_axis=0, concat_axis=2, tiled=True)
    attended = jnp.einsum("psc,cd->psd", moved, out_weight, preferred_element_type=jnp.float32)
    residual = input_values + attended
    normed_feed = rms_scale(residual, feed_gain, 1e-06).astype(jnp.bfloat16)
    gathered_feed = lax.all_gather(normed_feed, "hid", axis=0, tiled=True)
    feed_gate = jnp.einsum(
        "psd,df->psf", gathered_feed, feed_gate_weight, preferred_element_type=jnp.float32
    )
    feed_up = jnp.einsum(
        "psd,df->psf", gathered_feed, up_weight, preferred_element_type=jnp.float32
    )
    hidden = (jax.nn.silu(feed_gate) * feed_up).astype(jnp.bfloat16)
    picked = hidden
    feed_out = lax.psum_scatter(
        jnp.einsum("psf,fd->psd", picked, down_weight, preferred_element_type=jnp.float32),
        "hid",
        scatter_dimension=0,
        tiled=True,
    )
    output = (residual + feed_out).astype(jnp.bfloat16)
    grad_gathered = lax.all_gather(cotangent, "hid", axis=0, tiled=True)
    grad_hidden = jnp.einsum(
        "psd,fd->psf", grad_gathered, down_weight, preferred_element_type=jnp.float32
    )
    grad_down = jnp.einsum("psf,psd->fd", hidden, grad_gathered, preferred_element_type=jnp.float32)
    sigmoid_gate = jax.nn.sigmoid(feed_gate)
    grad_feed_gate = (
        grad_hidden * feed_up * sigmoid_gate * (1.0 + feed_gate * (1.0 - sigmoid_gate))
    ).astype(jnp.bfloat16)
    grad_feed_up = (grad_hidden * feed_gate * sigmoid_gate).astype(jnp.bfloat16)
    grad_feed_gate_w = jnp.einsum(
        "psd,psf->df", gathered_feed, grad_feed_gate, preferred_element_type=jnp.float32
    )
    grad_up_w = jnp.einsum(
        "psd,psf->df", gathered_feed, grad_feed_up, preferred_element_type=jnp.float32
    )
    grad_normed_feed = lax.psum_scatter(
        jnp.einsum(
            "psf,df->psd", grad_feed_gate, feed_gate_weight, preferred_element_type=jnp.float32
        )
        + jnp.einsum("psf,df->psd", grad_feed_up, up_weight, preferred_element_type=jnp.float32),
        "hid",
        scatter_dimension=0,
        tiled=True,
    )

    def feed_norm(values_in, gain_values):
        return rms_scale(values_in, gain_values, 1e-06)

    _, feed_pull = jax.vjp(feed_norm, residual, feed_gain)
    grad_resid_part, grad_feed_gain = feed_pull(grad_normed_feed)
    grad_residual = cotangent.astype(jnp.float32) + grad_resid_part
    grad_attended = grad_residual.astype(jnp.bfloat16)
    grad_gated_rows = jnp.einsum(
        "psd,cd->psc", grad_attended, out_weight, preferred_element_type=jnp.float32
    )
    grad_out = jnp.einsum("psc,psd->cd", moved, grad_attended, preferred_element_type=jnp.float32)
    grad_gated = lax.all_to_all(grad_gated_rows, "hid", split_axis=2, concat_axis=0, tiled=True)
    _, finish_pull = jax.vjp(head_finish, mixture, out_gate, head_gain)
    grad_mixture, grad_out_gate, grad_head = finish_pull(grad_gated)
    grad_blocks = grad_mixture.reshape(
        span_len // block_len, block_len, seq_count, heads_here, HDIM
    )
    block_ends = cumulative[:, block_len - 1 :]
    earlier_sum = jnp.cumsum(block_ends, axis=0) - block_ends
    reaching = jnp.einsum(
        "btshk,btshv->shkv",
        blocked[0] * jnp.exp(cumulative + earlier_sum),
        grad_blocks,
        precision=precise,
    )
    _, outgoing = entering(
        (device_fade, reaching), "seq", combine_states, (unity, zero_state), True
    )
    _, scan_pull = jax.vjp(recurrence, blocked[0], blocked[1], blocked[2], incoming)
    grad_queries, grad_rates, grad_values, _ = scan_pull((grad_blocks, outgoing))
    flat_shape = (span_len, seq_count, local_cols)
    _, rate_pull = jax.vjp(rate_of, forget_pre, lower_bound)
    grad_forget_pre, grad_lower = rate_pull(grad_rates.reshape(flat_shape))
    grad_joint = jnp.concatenate(
        [
            grad_queries.reshape(flat_shape),
            grad_forget_pre,
            grad_values.reshape(flat_shape),
            grad_out_gate,
        ],
        axis=2,
    ).astype(jnp.bfloat16)
    grad_joint_w = jnp.einsum(
        "psd,pse->de", gathered_in, grad_joint, preferred_element_type=jnp.float32
    )
    picked = grad_joint
    grad_normed_in = lax.psum_scatter(
        jnp.einsum("pse,de->psd", picked, joint_weight, preferred_element_type=jnp.float32),
        "hid",
        scatter_dimension=0,
        tiled=True,
    )

    def mixer_norm(values_in, gain_values):
        return rms_scale(values_in, gain_values, 1e-06)

    _, mixer_pull = jax.vjp(mixer_norm, input_values, mixer_gain)
    grad_input_part, grad_mixer = mixer_pull(grad_normed_in)
    grad_tokens = grad_residual + grad_input_part
    grad_query_w, grad_forget_w, grad_input_w, grad_gate_w = jnp.split(grad_joint_w, 4, axis=1)
    summed = lax.psum(
        (
            grad_query_w,
            grad_forget_w,
            grad_input_w,
            grad_gate_w,
            grad_lower,
            grad_head,
            grad_feed_gate_w,
            grad_up_w,
            grad_down,
        ),
        "seq",
    )
    shared = lax.psum((grad_mixer, grad_feed_gain, grad_out, forget_total), ("seq", "hid"))
    mean_forget = shared[3] / (model_width * jnp.sum(lengths).astype(jnp.float32))
    return (
        output,
        grad_tokens,
        shared[0],
        summed[0],
        summed[1],
        summed[2],
        summed[3],
        summed[4],
        summed[5],
        shared[2],
        shared[1],
        summed[6],
        summed[7],
        summed[8],
        mean_forget,
    )


def solution(mesh):
    placed = (
        P(("seq", "hid"), None, None),
        P(),
        P(("seq", "hid"), None, None),
        P(),
        P(None, "hid"),
        P(None, "hid"),
        P(None, "hid"),
        P(None, "hid"),
        P("hid"),
        P("hid"),
        P(),
        P(),
        P(None, "hid"),
        P(None, "hid"),
        P("hid", None),
    )
    return jax.shard_map(
        shards,
        mesh=mesh,
        in_specs=placed,
        out_specs=(
            P(("seq", "hid"), None, None),
            P(("seq", "hid"), None, None),
            P(),
            P(None, "hid"),
            P(None, "hid"),
            P(None, "hid"),
            P(None, "hid"),
            P("hid"),
            P("hid"),
            P(),
            P(),
            P(None, "hid"),
            P(None, "hid"),
            P("hid", None),
            P(),
        ),
        check_vma=False,
    )
```

profile of v0, /device:TPU:0, one launch (start us, length us, event | category | flops | bytes accessed | tf_op | source)
XLA Modules:
  0.0 2221.1 jit_solution(4145258278423627629)
XLA Ops:
  13.6 57.0 %all-gather.9.cloned.1.call-done = bf16[512,4,2048]{2,0,1:T(8,128)(2,1)} async-done(((bf16[64,4,2048]{2,0,1:T(8,128)(2,1)}), bf16[512,4,2048]{2,0,1:T(8,128)(2,1)}) %all-gather.9.cloned.1.call-update) | async-done | bytes 8388624 | tf_op jit(solution)/shard_map/all_gather | solution.py:102
  70.6 12.4 fusion.79
  100.4 13.0 fusion.75
  113.4 11.0 while.86
  128.5 13.4 all-gather
  142.0 11.3 fusion.104
  153.3 18.1 all-gather.15.cloned.1.call-done
  175.0 32.6 %while.82 = (s32[]{:T(128)}, f32[4,2,128,128]{3,2,1,0:T(8,128)}, f32[8,4,2,128,128]{4,3,2,1,0:T(8,128)}, f32[8,4,2,128]{3,2,1,0:T(2,128)S(1)}, f32[8,4,2,128,128]{4,3,2,1,0:T(8,128)}, /*index=5*/s32[]{:T(128)}) while((s32[]{:T(128)}, f32[4,2,128,128]{3,2,1,0:T(8,128)}, f32[8,4,2,128,128]{4,3,2,1,0:T(8,128)}, f32[8,4,2,128]{3,2,1,0:T(2,128)S(1)}, ...), condition=%wide.region_8.9_spmd, body=%wide.region_7.8_spmd.sunk | while | flops 262146 | bytes 2634317 | solution.py:62
  244.8 19.2 all_to_all.36
  280.6 52.6 %all-gather.11.cloned.1.call-done = bf16[512,4,2048]{2,0,1:T(8,128)(2,1)} async-done(((bf16[64,4,2048]{2,0,1:T(8,128)(2,1)}), bf16[512,4,2048]{2,0,1:T(8,128)(2,1)}) %all-gather.11.cloned.1.call-update) | async-done | bytes 8388624 | tf_op jit(solution)/shard_map/all_gather | solution.py:146
  333.2 11.2 fusion.10
  352.4 37.6 %all-gather.13.cloned.1.call-done = bf16[512,4,2048]{2,0,1:T(8,128)(2,1)} async-done(((bf16[64,4,2048]{2,0,1:T(8,128)(2,1)}), bf16[512,4,2048]{2,0,1:T(8,128)(2,1)}) %all-gather.13.cloned.1.call-update) | async-done | bytes 8388624 | tf_op jit(solution)/shard_map/all_gather | solution.py:162
  390.0 14.7 multiply_convert_fusion
  404.7 10.7 fusion.12
  415.4 13.9 convolution_add_fusion
  429.5 13.9 fusion.7
  443.4 102.1 %reduce-scatter.6.cloned.1.call-done = f32[64,4,2048]{2,0,1:T(8,128)} async-done(((f32[512,4,2048]{2,0,1:T(8,128)}), f32[64,4,2048]{2,0,1:T(8,128)}) %reduce-scatter.6.cloned.1.call-update) | async-done | bytes 2097168 | tf_op jit(solution)/shard_map/reduce_scatter | solution.py:178
  548.2 116.8 %reduce-scatter.4.cloned.1.call-done = f32[64,4,2048]{2,0,1:T(8,128)} async-done(((f32[512,4,2048]{2,0,1:T(8,128)}), f32[64,4,2048]{2,0,1:T(8,128)}) %reduce-scatter.4.cloned.1.call-update) | async-done | bytes 2097168 | tf_op jit(solution)/shard_map/reduce_scatter | solution.py:155
  691.8 26.2 %all-to-all-done.1 = f32[8,1,65536]{2,1,0:T(1,128)S(1)} async-done(((f32[8,1,65536]{2,1,0:T(1,128)}), f32[8,1,65536]{2,1,0:T(1,128)S(1)}, u32[]{:S(2)}, u32[]{:S(2)}) %all-to-all-start.1) | async-done | bytes 2097184 | tf_op jit(solution)/shard_map/all_to_all | solution.py:199
  758.9 17.8 while.83
  817.7 20.9 while.85
  838.6 15.0 fusion.107
  853.8 11.0 fusion.39
  902.8 16.8 fusion.78
  921.2 12.7 convolution_bitcast_fusion
  934.0 12.4 convolution_bitcast_fusion.2
  946.4 10.2 convolution_bitcast_fusion.3
  990.6 41.5 %reduce-scatter.8.cloned.1.call-done = f32[64,4,2048]{2,0,1:T(8,128)} async-done(((f32[512,4,2048]{2,0,1:T(8,128)}), f32[64,4,2048]{2,0,1:T(8,128)}) %reduce-scatter.8.cloned.1.call-update) | async-done | bytes 2097168 | tf_op jit(solution)/shard_map/reduce_scatter | solution.py:234
  1040.4 41.8 %all-reduce.2 = (f32[2048]{0:T(1024)}, f32[2048]{0:T(1024)}, f32[]{:T(128)}) all-reduce(f32[2048]{0:T(1024)S(1)} %get-tuple-element.456, f32[2048]{0:T(1024)S(1)} %copy-done.52, f32[]{:T(128)} %get-tuple-element.459), channel_id=1, replica_groups=mesh['seq'=4,'hid'=8] {'seq','hid'}, use_global_device_ids=true, to_apply=%region_30.31 | all-reduce | flops 4097 | bytes 32776 | tf_op jit(solution)/shard_map/psum | solution.py:262
  1082.8 234.4 %all-reduce.8.cloned.1.call-done = f32[2048,2048]{1,0:T(8,128)} async-done(((f32[2048,2048]{1,0:T(8,128)}), f32[2048,2048]{1,0:T(8,128)}) %all-reduce.8.cloned.1.call-update) | async-done | bytes 16777232 | tf_op jit(solution)/shard_map/psum | solution.py:262
  1317.2 862.0 %all-reduce.10.cloned.1.call-done = (f32[2048,256]{1,0:T(8,128)}, f32[2048,256]{1,0:T(8,128)}, f32[2048,256]{1,0:T(8,128)}, f32[2048,256]{1,0:T(8,128)}, f32[204...) async-done(((f32[2048,256]{1,0:T(8,128)}, f32[2048,256]{1,0:T(8,128)}, f32[2048,256]{1,0:T(8,128)}, f32[2048,256]{1,0:T(8,128)}, f32[2048,704]{0,1:T(8,128)}, ...) | async-done | bytes 25690128 | tf_op jit(solution)/shard_map/psum | solution.py:248
  2188.5 13.5 copy.404
  (413 shorter events, 392.5 us)
Async XLA Ops:
  7.2 382.8 %copy-start = (bf16[704,2048]{1,0:T(8,128)(2,1)S(1)}, bf16[704,2048]{1,0:T(8,128)(2,1)}, u32[]{:S(2)}) copy-start(bf16[704,2048]{1,0:T(8,128)(2,1)} %param.41) | copy-start | bytes 8650756
  7.2 63.4 %all-gather.9.cloned.1.call-start = ((), (), s32[]{:S(2)}) async-start(), calls=%async_computation.5 | async-start | bytes 9437184 | tf_op jit(solution)/shard_map/all_gather | solution.py:102
  13.4 158.0 %all-gather.15.cloned.1.call-start = ((), (), s32[]{:S(2)}) async-start(), calls=%async_computation.12 | async-start | bytes 2621440 | tf_op jit(solution)/shard_map/all_gather | solution.py:18
  13.5 69.6 %copy-start.59 = (f32[256]{0:T(256)}, f32[256]{0:T(256)S(1)}, u32[]{:S(2)}) copy-start(f32[256]{0:T(256)S(1)} %broadcast_subtract_fusion) | copy-start | bytes 3076
  125.2 208.1 %all-gather.11.cloned.1.call-start = ((), (), s32[]{:S(2)}) async-start(), calls=%async_computation.6 | async-start | bytes 9437184 | tf_op jit(solution)/shard_map/all_gather | solution.py:146
  277.7 112.3 %all-gather.13.cloned.1.call-start = ((), (), s32[]{:S(2)}) async-start(), calls=%async_computation.8 | async-start | bytes 9437184 | tf_op jit(solution)/shard_map/all_gather | solution.py:162
  280.5 265.0 %reduce-scatter.6.cloned.1.call-start = ((), (), s32[]{:S(2)}) async-start(), calls=%async_computation.9 | async-start | bytes 18874368 | tf_op jit(solution)/shard_map/reduce_scatter | solution.py:178
  429.4 235.5 %reduce-scatter.4.cloned.1.call-start = ((), (), s32[]{:S(2)}) async-start(), calls=%async_computation.7 | async-start | bytes 18874368 | tf_op jit(solution)/shard_map/reduce_scatter | solution.py:155
  443.4 102.2 %copy-start.24 = (f32[64,4,2048]{2,0,1:T(8,128)S(1)}, f32[64,4,2048]{2,0,1:T(8,128)}, u32[]{:S(2)}) copy-start(f32[64,4,2048]{2,0,1:T(8,128)} %copy-done.23) | copy-start | bytes 6291460
  443.4 102.2 %copy-start.54 = (f32[64,4]{0,1:T(4,128)S(1)}, f32[64,4]{0,1:T(4,128)}, u32[]{:S(2)}) copy-start(f32[64,4]{0,1:T(4,128)} %copy-done.53) | copy-start | bytes 3076
  443.4 104.8 %copy-start.64 = (f32[64,4]{0,1:T(4,128)S(1)}, f32[64,4]{0,1:T(4,128)}, u32[]{:S(2)}) copy-start(f32[64,4]{0,1:T(4,128)} %copy-done.63) | copy-start | bytes 3076
  687.6 30.3 %all-to-all-start.1 = ((f32[8,1,65536]{2,1,0:T(1,128)}), f32[8,1,65536]{2,1,0:T(1,128)S(1)}, u32[]{:S(2)}, u32[]{:S(2)}) async-start(f32[8,1,65536]{2,1,0:T(1,128)} %reshape.251), calls=%async_computation.3 | async-start | bytes 4194304 | tf_op jit(solution)/shard_map/all_to_all | solution.py:199
  691.4 117.6 %all-gather.17.cloned.1.call-start = ((), (), s32[]{:S(2)}) async-start(), calls=%async_computation.13 | async-start | bytes 2621440 | tf_op jit(solution)/shard_map/all_gather | solution.py:18
  756.3 275.8 %reduce-scatter.8.cloned.1.call-start = ((), (), s32[]{:S(2)}) async-start(), calls=%async_computation.10 | async-start | bytes 18874368 | tf_op jit(solution)/shard_map/reduce_scatter | solution.py:234
  817.6 20.9 copy-start.39
  838.6 15.1 copy-start.5
  838.6 15.1 copy-start.8
  838.6 15.1 copy-start.12
  838.6 15.1 copy-start.15
  838.6 15.1 copy-start.16
  838.6 15.1 copy-start.25
  919.6 397.6 %all-reduce.8.cloned.1.call-start = ((), (), s32[]{:S(2)}) async-start(), calls=%async_computation.11 | async-start | bytes 33554432 | tf_op jit(solution)/shard_map/psum | solution.py:262
  933.9 1245.3 %all-reduce.10.cloned.1.call-start = ((), (), s32[]{:S(2)}) async-start(), calls=%async_computation.14 | async-start | bytes 51380224 | tf_op jit(solution)/shard_map/psum | solution.py:248
  934.0 22.6 %slice-start.8 = ((s8[8388608]{0:T(1024)(128)(4,1)}), s8[4194304]{0:T(1024)(128)(4,1)S(1)}, s32[]{:S(2)}) async-start(s8[8388608]{0:T(1024)(128)(4,1)} %bitcast.285), calls=%async_computation.23 | async-start | bytes 8388608
  946.4 18.5 slice-start.6
  978.4 53.7 %copy-start.27 = (bf16[64,4,2048]{2,1,0:T(4,128)(2,1)S(1)}, bf16[64,4,2048]{2,1,0:T(4,128)(2,1)}, u32[]{:S(2)}) copy-start(bf16[64,4,2048]{2,1,0:T(4,128)(2,1)} %param.27) | copy-start | bytes 3145732
  978.4 53.7 %copy-start.51 = (f32[2048]{0:T(1024)S(1)}, f32[2048]{0:T(1024)}, u32[]{:S(2)}) copy-start(f32[2048]{0:T(1024)} %param.30) | copy-start | bytes 24580
  978.4 53.7 %copy-start.56 = (f32[64,4]{0,1:T(4,128)S(1)}, f32[64,4]{0,1:T(4,128)}, u32[]{:S(2)}) copy-start(f32[64,4]{0,1:T(4,128)} %copy-done.55) | copy-start | bytes 3076
  981.5 53.5 %copy-start.58 = (f32[64,4]{0,1:T(4,128)S(1)}, f32[64,4]{0,1:T(4,128)}, u32[]{:S(2)}) copy-start(f32[64,4]{0,1:T(4,128)} %copy-done.57) | copy-start | bytes 3076
  2187.1 14.8 slice-start.4
  2187.1 17.7 slice-start.2
  2188.5 16.4 slice-start.3
  (67 other events, 361.0 us)
Sparse Core Ops, SparseCore 0:
  13.5 57.0 all-gather.8
  125.3 46.0 all-gather.14
  277.8 55.3 all-gather.10
  335.6 54.3 all-gather.12
  429.5 115.9 reduce-scatter.5
  548.9 115.9 reduce-scatter.3
  756.4 45.0 all-gather.16
  919.8 112.3 reduce-scatter.7
  1038.2 279.0 all-reduce.7
  1321.7 857.5 all-reduce.9
where the time goes:
time: 2230 us; the launch traced here: 2220 us
  waiting for transfers between devices  1550 us (70%)
  matrix products  276 us (12%)
  local copies, waits for them, and re-layouts  174 us (8%)
  other arithmetic  116 us (5%)
  blocking collectives  83.5 us (4%)
    psum x1, waiting for transfers between devices, shards(): lax.psum((grad_query_w, grad_forget_w, grad_input_w, grad_gate_w, grad_lo...  862 us
    psum x1, waiting for transfers between devices, shards(): lax.psum((grad_mixer, grad_feed_gain, grad_out, forget_total), ('seq', 'h...  234 us
    reduce_scatter x1, waiting for transfers between devices, shards(): lax.psum_scatter(jnp.einsum('psf,fd->psd', picked, down_weight, preferred...  117 us
    reduce_scatter x1, waiting for transfers between devices, shards(): lax.psum_scatter(jnp.einsum('psf,df->psd', grad_feed_gate, feed_gate_weig...  102 us
    unnamed x191, local copies, waits for them, and re-layouts  70.1 us
    all_gather x1, waiting for transfers between devices, shards(): gathered_in = lax.all_gather(normed_in, 'hid', axis=0, tiled=True)  57 us
    all_gather x1, waiting for transfers between devices, shards(): gathered_feed = lax.all_gather(normed_feed, 'hid', axis=0, tiled=True)  52.6 us
  transfers between devices with their start and end apart: 11, of which 10 were waited for; matrix products, arithmetic and copies ran while one was open for 8% of the time, Pallas kernels for 0%

commit v1 on v0

v1 whole, which is shorter than its diff:
```python
import functools

import jax
import jax.numpy as jnp
import numpy as np
from jax import lax
from jax.experimental import pallas as pl
from jax.experimental.pallas import tpu as pltpu
from jax.sharding import PartitionSpec as P

HDIM = 128
F32 = jnp.float32
BF = jnp.bfloat16
VMEM = 60 * 1024 * 1024

NN = (((1,), (0,)), ((), ()))
NT = (((1,), (1,)), ((), ()))
TN = (((0,), (0,)), ((), ()))


def dot(a, b, dims):
    return lax.dot_general(a, b, dims, preferred_element_type=F32)


def halves(a):
    high = a.astype(BF)
    return high, (a - high.astype(F32)).astype(BF)


def dot3(a, b, dims):
    ah, al = halves(a)
    bh, bl = halves(b)
    return dot(ah, bh, dims) + (dot(ah, bl, dims) + dot(al, bh, dims))


def summed(mask, a):
    high, rest = halves(a)
    ones = mask.astype(BF)
    return dot(ones, high, NN) + dot(ones, rest, NN)


def tie(x, *after):
    return lax.optimization_barrier((x, after))[0]


def hop(array, mask):
    count = lax.axis_size("hid")
    return lax.ppermute(array, "hid", [(i, i ^ mask) for i in range(count)])


def masks(count):
    links = [1 << b for b in range(1, count.bit_length() - 1)]
    return [1] + links, [1] + links[1:] + links[:1]


def b_offsets(count):
    _, mask_b = masks(count)
    table = np.zeros(count, np.int32)
    for t in range(count):
        for bit, mask in enumerate(mask_b):
            if t >> bit & 1:
                table[t] ^= mask
    return table


class Gather:
    def __init__(self, a, b):
        self.mask_a, self.mask_b = masks(lax.axis_size("hid"))
        self.a, self.b = a[None], b[None]

    def links(self, last, after=()):
        bits = range(1, len(self.mask_a))[-1:] if last else range(1, len(self.mask_a) - 1)
        for bit in bits:
            a, b = (tie((self.a, self.b), *after) if after else (self.a, self.b))
            got_a, got_b = hop(a, self.mask_a[bit]), hop(b, self.mask_b[bit])
            if last:
                self.late = (got_a, got_b)
            else:
                self.a = jnp.concatenate([self.a, got_a])
                self.b = jnp.concatenate([self.b, got_b])

    def early(self):
        return [self.a, self.b, hop(self.a, 1), hop(self.b, 1)]

    def other(self, after=()):
        sent = tie(self.late, *after) if after else self.late
        return [hop(x, 1) for x in sent]


class Scatter:
    def __init__(self, odd):
        self.count = lax.axis_size("hid")
        self.masks = masks(self.count)
        self.got = hop(odd, 1)

    def first(self, even):
        self.kept = [[even[ab], self.got[ab]] for ab in range(2)]
        self.bit = len(self.masks[0]) - 1
        return self.step()

    def step(self):
        half = self.kept[0][0].shape[0] // 2
        sends = [
            sum(x[half:].astype(F32) for x in kept).astype(BF) for kept in self.kept
        ]
        got = [hop(send, mask[self.bit]) for send, mask in zip(sends, self.masks)]
        self.kept = [[x[:half] for x in kept] + [g] for kept, g in zip(self.kept, got)]
        self.bit -= 1
        return sends

    def more(self):
        return self.bit >= 1

    def result(self):
        return jnp.concatenate(
            [sum(x[0].astype(F32) for x in kept) for kept in self.kept], axis=0
        )


class Sums:
    def __init__(self):
        count = lax.axis_size("seq")
        half = count // 2
        self.place = lax.axis_index("seq")
        inward = [[(i, i + 1), (count - 1 - i, count - 2 - i)] for i in range(half - 1)]
        middle = [[(half - 1, half), (half, half - 1)]]
        self.pairs = inward + middle + [[(b, a) for a, b in pair] for pair in inward[::-1]]
        self.adding = half
        self.last = [None] * len(self.pairs)
        self.flying = []
        self.count = count

    def start(self, piece, stage):
        value = piece["total"]
        if self.last[stage] is not None:
            value = tie(value, self.last[stage])
        piece["got"] = self.last[stage] = lax.ppermute(value, "seq", self.pairs[stage])
        piece["stage"] = stage

    def push(self, value):
        piece = {"total": value}
        self.start(piece, 0)
        self.flying.append(piece)
        return piece

    def tick(self, line):
        for piece in list(self.flying)[::-1]:
            self.turn(piece, line)

    def turn(self, piece, line):
        stage = piece["stage"]
        total, got = piece["total"], piece["got"]
        if stage < self.adding:
            total = line(lambda a, b: (a.astype(F32) + b.astype(F32)).astype(BF), total, got)
        else:
            (target, other) = [b for _, b in self.pairs[stage]]
            mine = (self.place == target) | (self.place == other)
            if stage + 1 < len(self.pairs):
                total = line(lambda a, b: jnp.where(mine, b, a), total, got)
            else:
                total = jnp.where(mine, got, total)
        piece["total"] = total
        if stage + 1 < len(self.pairs):
            self.start(piece, stage + 1)
        else:
            self.flying.remove(piece)

    def drain(self, line):
        while self.flying:
            self.tick(line)


class Line:
    def __init__(self):
        self.token = None

    def __call__(self, function, *args):
        if self.token is not None:
            args = tie(args, self.token)
        result = function(*args)
        self.token = jax.tree.leaves(result)[0]
        return result


def everywhere(value, axis):
    count = lax.axis_size(axis)
    mask = 1
    while mask < count:
        value = value + lax.ppermute(value, axis, [(i, i ^ mask) for i in range(count)])
        mask *= 2
    return value


class Entering:
    def __init__(self, state, fade, reverse):
        self.count = lax.axis_size("seq")
        self.reverse = reverse
        self.reach, self.cover, self.fade = 1, state, fade
        self.border = None
        self.send()

    def send(self):
        step = -self.reach if self.reverse else self.reach
        pairs = [(i, i + step) for i in range(self.count) if 0 <= i + step < self.count]
        self.got = [
            lax.ppermute(self.cover.astype(BF), "seq", pairs),
            lax.ppermute(self.fade, "seq", pairs),
        ]

    def take(self, line):
        def merge(got, got_fade, cover, fade, border, border_fade):
            got = got.astype(F32)
            if border is None:
                border, border_fade = got, got_fade
            else:
                border, border_fade = border + border_fade * got, border_fade * got_fade
            return border, border_fade, cover + fade * got, fade * got_fade

        border = self.border or (None, None)
        *self.border, self.cover, self.fade = line(
            merge, *self.got, self.cover, self.fade, *border
        )
        self.reach *= 2
        if self.reach >= self.count:
            return True
        self.send()
        return False

    def finish(self, line):
        while not self.take(line):
            pass
        return self.border[0]


def stream(groups, place, count, weights, outs, body, before=None):
    chips, rows, width = groups[0][0].shape
    n_sets, n_w, n_out = len(groups), len(weights), len(outs)
    parts = len(groups[0])
    n_arrays = parts * n_sets
    steps = chips if place is None else 1
    lines = 4 * rows if place is None else chips * 2 * rows

    def kernel(*refs):
        arrays = refs[:n_arrays]
        w_refs = refs[n_arrays : n_arrays + n_w]
        refs = refs[n_arrays + n_w + (n_out if before is not None else 0) :]
        out_refs, bufs, sem = refs[:n_out], refs[n_out:-1], refs[-1]
        i = pl.program_id(0)

        def copies(k):
            chosen = [(k, part, part) for part in range(4)]
            if place is not None:
                chosen = [(c, ab, 2 * c + ab) for c in range(chips) for ab in range(2)]
            return [
                pltpu.make_async_copy(
                    arrays[parts * s + part].at[c],
                    bufs[s].at[k % 2, pl.ds(at * rows, rows)],
                    sem.at[s, k % 2, at],
                )
                for s in range(n_sets)
                for c, part, at in chosen
            ]

        for k in range(steps):

            @pl.when(i == k)
            def _(k=k):
                if k == 0:
                    for copy in copies(0):
                        copy.start()
                if k + 1 < steps:
                    for copy in copies(k + 1):
                        copy.start()
                for copy in copies(k):
                    copy.wait()

        slot = lax.rem(i, 2) if steps > 1 else 0
        results = body([buf[slot] for buf in bufs], w_refs)
        for ref, value in zip(out_refs, results):
            ref[...] = value.reshape(ref.shape).astype(ref.dtype)

    anywhere = pl.BlockSpec(memory_space=pl.ANY)
    whole = lambda w: pl.BlockSpec(w.shape, lambda i: (0, 0), pipeline_mode=pl.Buffered(1))
    given = [] if before is None else list(before)
    if place is None:
        out_spec = lambda c: pl.BlockSpec((1, 2, 2, rows, c), lambda i: (i, 0, 0, 0, 0))
    else:
        out_spec = lambda c: pl.BlockSpec((chips, 1, 2, rows, c), lambda i: (1, place, 0, 0, 0))
    return pl.pallas_call(
        kernel,
        grid=(steps,),
        in_specs=[anywhere] * n_arrays + [whole(w) for w in weights] + [anywhere] * len(given),
        out_specs=[out_spec(c) for c, _ in outs],
        out_shape=[jax.ShapeDtypeStruct((count // 2, 2, 2, rows, c), d) for c, d in outs],
        scratch_shapes=[pltpu.VMEM((min(steps, 2), lines, width), BF) for _ in groups]
        + [pltpu.SemaphoreType.DMA((n_sets, 2, lines // rows))],
        input_output_aliases={n_arrays + n_w + o: o for o in range(len(given))},
        compiler_params=pltpu.CompilerParams(vmem_limit_bytes=VMEM),
    )(*[x for s in groups for x in s], *weights, *given)


def by_slot(arrays):
    return [x.reshape((-1,) + x.shape[2:]) for x in arrays]


def head_rows(rows, out_weight, count):
    own, width = rows.shape
    cols = out_weight.shape[0] // count

    def kernel(rows_ref, weight_ref, out_ref):
        out_ref[0] = dot(rows_ref[...], weight_ref[...], NT).astype(BF)

    return pl.pallas_call(
        kernel,
        grid=(count,),
        in_specs=[
            pl.BlockSpec((own, width), lambda i: (0, 0)),
            pl.BlockSpec((cols, width), lambda i: (i, 0)),
        ],
        out_specs=pl.BlockSpec((1, own, cols), lambda i: (i, 0, 0)),
        out_shape=jax.ShapeDtypeStruct((count, own, cols), BF),
        compiler_params=pltpu.CompilerParams(vmem_limit_bytes=VMEM),
    )(rows, out_weight)


def partial_rows(lefts, weights, dims, parity):
    count, _, rows, _ = lefts[0].shape
    width = weights[0].shape[1 if dims == NN else 0]
    n = len(lefts)

    def kernel(*refs):
        total = None
        for left, weight in zip(refs[:n], refs[n : 2 * n]):
            value = left[...].reshape(2 * rows, left.shape[-1])
            part = dot(value, weight[...], dims)
            total = part if total is None else total + part
        refs[2 * n][...] = total.astype(BF).reshape(2, 1, rows, width)

    whole = lambda w: pl.BlockSpec(w.shape, lambda i: (0, 0), pipeline_mode=pl.Buffered(1))
    return pl.pallas_call(
        kernel,
        grid=(count // 2,),
        in_specs=[
            pl.BlockSpec((1, 2, rows, x.shape[-1]), lambda i: (2 * i + parity, 0, 0, 0))
            for x in lefts
        ]
        + [whole(w) for w in weights],
        out_specs=pl.BlockSpec((2, 1, rows, width), lambda i: (0, i, 0, 0)),
        out_shape=jax.ShapeDtypeStruct((2, count // 2, rows, width), BF),
        compiler_params=pltpu.CompilerParams(vmem_limit_bytes=VMEM),
    )(*lefts, *weights)


def owned_rows(left, weight, table):
    count, _, rows, depth = left.shape
    width = weight.shape[1]

    def kernel(_, left_ref, weight_ref, a_ref, b_ref):
        total = dot(left_ref[...].reshape(2 * rows, depth), weight_ref[...], NN).astype(BF)
        a_ref[...] = total[:rows]
        b_ref[...] = total[rows:]

    return pl.pallas_call(
        kernel,
        grid_spec=pltpu.PrefetchScalarGridSpec(
            num_scalar_prefetch=1,
            grid=(count,),
            in_specs=[
                pl.BlockSpec((1, 2, rows, depth), lambda t, tab: (t, 0, 0, 0)),
                pl.BlockSpec(weight.shape, lambda t, tab: (0, 0), pipeline_mode=pl.Buffered(1)),
            ],
            out_specs=[
                pl.BlockSpec((rows, width), lambda t, tab: (tab[t], 0)),
                pl.BlockSpec((rows, width), lambda t, tab: (tab[count + t], 0)),
            ],
        ),
        out_shape=[jax.ShapeDtypeStruct((count * rows, width), BF)] * 2,
        compiler_params=pltpu.CompilerParams(vmem_limit_bytes=VMEM),
    )(table, left, weight)


def attend(moved, out_weight, own_rows, gain):
    count, rows, cols = moved.shape
    depth, width = out_weight.shape
    block = 512
    steps = width // block

    def kernel(moved_ref, weight_ref, own_ref, gain_ref, res_ref, normed_ref, left_ref):
        i = pl.program_id(0)

        @pl.when(i == 0)
        def _():
            for s in range(count):
                left_ref[:, s * cols : (s + 1) * cols] = moved_ref[s]

        part = dot(left_ref[...], weight_ref[...], NN)
        for k in range(steps):

            @pl.when(i == k)
            def _(k=k):
                at = slice(k * block, (k + 1) * block)
                res_ref[:, at] = own_ref[:, at].astype(F32) + part

        @pl.when(i == steps - 1)
        def _():
            value = res_ref[...]
            scale = lax.rsqrt(jnp.mean(value * value, axis=-1, keepdims=True) + 1e-06)
            normed_ref[...] = (value * scale * gain_ref[...]).astype(BF)

    return pl.pallas_call(
        kernel,
        grid=(steps,),
        in_specs=[
            pl.BlockSpec((count, rows, cols), lambda i: (0, 0, 0)),
            pl.BlockSpec((depth, block), lambda i: (0, i)),
            pl.BlockSpec((rows, width), lambda i: (0, 0)),
            pl.BlockSpec((1, width), lambda i: (0, 0)),
        ],
        out_specs=[pl.BlockSpec((rows, width), lambda i: (0, 0))] * 2,
        out_shape=[
            jax.ShapeDtypeStruct((rows, width), F32),
            jax.ShapeDtypeStruct((rows, width), BF),
        ],
        scratch_shapes=[pltpu.VMEM((rows, depth), BF)],
        compiler_params=pltpu.CompilerParams(vmem_limit_bytes=VMEM),
    )(moved, out_weight, own_rows, gain)


class Scan:
    def __init__(self, count, seqs, rows, cols, table, base, lengths, lower):
        self.count, self.rows, self.cols = count, rows, cols
        self.per = seqs // 2
        self.heads = cols // HDIM
        self.total = seqs * self.heads
        self.scalars = jnp.concatenate([table, base[None], lengths]).astype(jnp.int32)
        self.lower = lower.reshape(1, cols)

    def slots(self, part, width, reverse):
        n = self.count

        def of(ab):
            def place(p, sc):
                p = n - 1 - p if reverse else p
                return (sc[ab * n + p], ab, 0, part)

            return pl.BlockSpec((1, 1, self.per * self.rows, width), place)

        return [of(0), of(1)]

    def chunk(self, shape, reverse):
        n = self.count
        zeros = (0,) * (len(shape) - 1)
        return pl.BlockSpec(
            (1,) + tuple(shape[1:]), lambda p, sc: ((n - 1 - p if reverse else p),) + zeros
        )

    def whole(self, shape):
        zeros = (0,) * len(shape)
        return pl.BlockSpec(tuple(shape), lambda p, sc: zeros)

    def call(self, kernel, in_specs, out_specs, out_shape, scratch, args):
        return pl.pallas_call(
            kernel,
            grid_spec=pltpu.PrefetchScalarGridSpec(
                num_scalar_prefetch=1,
                grid=(self.count,),
                in_specs=in_specs,
                out_specs=out_specs,
                scratch_shapes=scratch,
            ),
            out_shape=out_shape,
            compiler_params=pltpu.CompilerParams(vmem_limit_bytes=VMEM),
        )(self.scalars, *args)

    def units(self):
        for ab in range(2):
            for s in range(self.per):
                yield ab, s, slice(s * self.rows, (s + 1) * self.rows)

    def state(self, ab, s, h):
        return (ab * self.per + s) * self.heads + h

    def valid(self, sc, p, ab, s):
        n = self.count
        pos = sc[2 * n] + p * self.rows + lax.broadcasted_iota(jnp.int32, (self.rows, 1), 0)
        return (pos < sc[2 * n + 1 + ab * self.per + s]).astype(F32)

    def triangle(self):
        r = lax.broadcasted_iota(jnp.int32, (self.rows, self.rows), 0)
        c = lax.broadcasted_iota(jnp.int32, (self.rows, self.rows), 1)
        return r >= c, r <= c

    def rates(self, forget, lower, valid):
        negative = jax.nn.sigmoid(-forget)
        keys = valid * (1.0 - lower) * negative
        down, _ = self.triangle()
        cum = summed(down.astype(F32), jnp.log(1.0 - keys))
        return negative, keys, cum

    def ends(self, joint):
        n, total, c = self.count, self.total, self.cols

        def kernel(sc, fa_ref, fb_ref, va_ref, vb_ref, lower_ref, end_ref, fade_ref, sum_ref):
            p = pl.program_id(0)

            @pl.when(p == 0)
            def _():
                end_ref[...] = jnp.zeros(end_ref.shape, F32)
                fade_ref[...] = jnp.ones(fade_ref.shape, F32)
                sum_ref[...] = jnp.zeros(sum_ref.shape, F32)

            gates = jnp.zeros((1, c), F32)
            for ab, s, sp in self.units():
                f_ref, v_ref = (fa_ref, fb_ref)[ab], (va_ref, vb_ref)[ab]
                valid = self.valid(sc, p, ab, s)
                _, keys, cum = self.rates(f_ref[0, 0, sp], lower_ref[...], valid)
                last = cum[self.rows - 1 :]
                gates += jnp.sum(valid * (1.0 - keys), axis=0, keepdims=True)
                to_end = keys * jnp.exp(last - cum)
                fade = jnp.exp(last)
                values = v_ref[0, 0, sp]
                for h in range(self.heads):
                    at = self.state(ab, s, h)
                    ch = slice(h * HDIM, (h + 1) * HDIM)
                    grown = dot3(values[:, ch], to_end[:, ch], TN)
                    end_ref[at] = end_ref[at] * fade[:, ch] + grown
                    fade_ref[at] = fade_ref[at] * fade[:, ch]
            sum_ref[...] += gates

        shapes = [
            jax.ShapeDtypeStruct((total, HDIM, HDIM), F32),
            jax.ShapeDtypeStruct((total, 1, HDIM), F32),
            jax.ShapeDtypeStruct((1, c), F32),
        ]
        return self.call(
            kernel,
            self.slots(1, c, False) + self.slots(2, c, False) + [self.whole((1, c))],
            [self.whole(x.shape) for x in shapes],
            shapes,
            [],
            (joint,) * 4 + (self.lower,),
        )

    def forward(self, joint):
        n, total, c = self.count, self.total, self.cols
        rows = self.per * self.rows

        def kernel(sc, ja_ref, jb_ref, lower_ref, mix_ref, reach_ref, start_ref, fade_ref, state_ref, kept_ref):
            p = pl.program_id(0)

            @pl.when(p == 0)
            def _():
                state_ref[...] = jnp.zeros(state_ref.shape, F32)
                kept_ref[...] = jnp.ones(kept_ref.shape, F32)

            down, _ = self.triangle()
            mid_row = self.rows // 2 - 1
            for ab, s, sp in self.units():
                joint_ref = (ja_ref, jb_ref)[ab]
                valid = self.valid(sc, p, ab, s)
                queries = joint_ref[0, 0, sp, 0:c]
                values = joint_ref[0, 0, sp, 2 * c : 3 * c]
                _, keys, cum = self.rates(joint_ref[0, 0, sp, c : 2 * c], lower_ref[...], valid)
                mid, last = cum[mid_row : mid_row + 1], cum[self.rows - 1 :]
                q_mid = queries * jnp.exp(cum - mid)
                k_mid = keys * jnp.exp(mid - cum)
                q_start = q_mid * jnp.exp(mid)
                to_end = k_mid * jnp.exp(last - mid)
                fade = jnp.exp(last)
                for h in range(self.heads):
                    at = self.state(ab, s, h)
                    ch = slice(h * HDIM, (h + 1) * HDIM)
                    state, kept = state_ref[at], kept_ref[at]
                    start_ref[0, at] = state
                    fade_ref[0, at] = kept
                    scores = jnp.where(down, dot3(q_mid[:, ch], k_mid[:, ch], NT), 0.0)
                    mix = dot3(scores, values[:, ch], NN) + dot3(q_start[:, ch], state, NT)
                    state_ref[at] = state * fade[:, ch] + dot3(values[:, ch], to_end[:, ch], TN)
                    mix_ref[0, ab, sp, ch] = mix
                    reach_ref[0, ab, sp, ch] = q_start[:, ch] * kept
                    kept_ref[at] = kept * fade[:, ch]

        shapes = [
            jax.ShapeDtypeStruct((n, 2, rows, c), F32),
            jax.ShapeDtypeStruct((n, 2, rows, c), F32),
            jax.ShapeDtypeStruct((n, total, HDIM, HDIM), F32),
            jax.ShapeDtypeStruct((n, total, 1, HDIM), F32),
        ]
        return self.call(
            kernel,
            self.slots(0, 4 * c, False) + [self.whole((1, c))],
            [self.chunk(x.shape, False) for x in shapes],
            shapes,
            [pltpu.VMEM((total, HDIM, HDIM), F32), pltpu.VMEM((total, 1, HDIM), F32)],
            (joint, joint, self.lower),
        )

    def finish(self, joint, mixture, reach, initial, head_gain):
        n, total, c = self.count, self.total, self.cols
        rows = self.per * self.rows

        def kernel(sc, ga_ref, gb_ref, local_ref, reach_ref, init_ref, gain_ref, mix_ref, out_ref):
            p = pl.program_id(0)
            for ab, s, sp in self.units():
                gates = (ga_ref, gb_ref)[ab][0, 0, sp]
                valid = self.valid(sc, p, ab, s)
                scale = gain_ref[...] * (gates * jax.nn.sigmoid(gates)) * valid
                for h in range(self.heads):
                    at = self.state(ab, s, h)
                    ch = slice(h * HDIM, (h + 1) * HDIM)
                    mix = local_ref[0, ab, sp, ch] + dot3(reach_ref[0, ab, sp, ch], init_ref[at], NT)
                    rho = lax.rsqrt(jnp.mean(mix * mix, axis=-1, keepdims=True) + 1e-05)
                    mix_ref[0, ab, sp, ch] = mix
                    out_ref[0, ab, sp, ch] = (mix * rho * scale[:, ch]).astype(BF)

        shapes = [
            jax.ShapeDtypeStruct((n, 2, rows, c), F32),
            jax.ShapeDtypeStruct((n, 2, rows, c), BF),
        ]
        chunk = self.chunk(mixture.shape, False)
        return self.call(
            kernel,
            self.slots(3, c, False)
            + [chunk, chunk, self.whole((total, HDIM, HDIM)), self.whole((1, c))],
            [chunk, chunk],
            shapes,
            [],
            (joint, joint, mixture, reach, initial, head_gain.reshape(1, c)),
        )

    def finish_back(self, joint, mixture, grad_gated, head_gain):
        n, total, c = self.count, self.total, self.cols
        rows = self.per * self.rows

        def kernel(
            sc, qa_ref, qb_ref, fa_ref, fb_ref, ga_ref, gb_ref, mix_ref, grad_ref,
            lower_ref, gain_ref, gm_ref, gate_ref, head_ref, reach_ref,
        ):
            step = pl.program_id(0)
            p = n - 1 - step

            @pl.when(step == 0)
            def _():
                head_ref[...] = jnp.zeros(head_ref.shape, F32)
                reach_ref[...] = jnp.zeros(reach_ref.shape, F32)

            gain = gain_ref[...]
            heads = [jnp.zeros((1, HDIM), F32)] * self.heads
            for ab, s, sp in self.units():
                q_ref, f_ref, g_ref = (qa_ref, qb_ref)[ab], (fa_ref, fb_ref)[ab], (ga_ref, gb_ref)[ab]
                slot = sc[ab * n + p]
                valid = self.valid(sc, p, ab, s)
                _, _, cum = self.rates(f_ref[0, 0, sp], lower_ref[...], valid)
                q_start = q_ref[0, 0, sp] * jnp.exp(cum)
                fade = jnp.exp(cum[self.rows - 1 :])
                gates = g_ref[0, 0, sp]
                sig = jax.nn.sigmoid(gates)
                arriving = grad_ref[0, ab, sp].astype(F32) * valid
                e = arriving * (gates * sig)
                slope = arriving * gain * sig * (1.0 + gates * (1.0 - sig))
                for h in range(self.heads):
                    at = self.state(ab, s, h)
                    ch = slice(h * HDIM, (h + 1) * HDIM)
                    mix = mix_ref[0, ab, sp, ch]
                    rho = lax.rsqrt(jnp.mean(mix * mix, axis=-1, keepdims=True) + 1e-05)
                    scaled = mix * rho
                    heads[h] += jnp.sum(e[:, ch] * scaled, axis=0, keepdims=True)
                    ge = gain[:, ch] * e[:, ch]
                    gm = rho * ge - mix * (rho * rho * rho) * jnp.mean(
                        mix * ge, axis=-1, keepdims=True
                    )
                    gm_ref[0, ab, sp, ch] = gm
                    gate_ref[slot, ab, sp, ch] = (scaled * slope[:, ch]).astype(BF)
                    reach_ref[at] = reach_ref[at] * fade[:, ch] + dot3(gm, q_start[:, ch], TN)
            for h in range(self.heads):
                head_ref[:, h * HDIM : (h + 1) * HDIM] += heads[h]

        shapes = [
            jax.ShapeDtypeStruct((n, 2, rows, c), F32),
            jax.ShapeDtypeStruct((n, 2, rows, c), BF),
            jax.ShapeDtypeStruct((1, c), F32),
            jax.ShapeDtypeStruct((total, HDIM, HDIM), F32),
        ]
        slots = lambda part: self.slots(part, c, True)
        return self.call(
            kernel,
            slots(0) + slots(1) + slots(3)
            + [self.chunk(mixture.shape, True), self.chunk(mixture.shape, True)]
            + [self.whole((1, c)), self.whole((1, c))],
            [self.chunk(shapes[0].shape, True)] + [self.whole(x.shape) for x in shapes[1:]],
            shapes,
            [],
            (joint,) * 6 + (mixture, grad_gated, self.lower, head_gain.reshape(1, c)),
        )

    def backward(self, joint, grad_mix, starts, fades, initial, final, leaving):
        n, total, c = self.count, self.total, self.cols
        rows = self.per * self.rows

        def kernel(
            sc, qa_ref, qb_ref, fa_ref, fb_ref, va_ref, vb_ref, gm_ref, start_ref, fade_ref,
            init_ref, final_ref, leave_ref, lower_ref, out_ref, low_ref, back_ref, end_ref,
        ):
            step = pl.program_id(0)
            p = n - 1 - step

            @pl.when(step == 0)
            def _():
                back_ref[...] = leave_ref[...]
                end_ref[...] = final_ref[...]
                low_ref[...] = jnp.zeros(low_ref.shape, F32)

            down, up = self.triangle()
            mid_row = self.rows // 2 - 1
            room = 1.0 - lower_ref[...]
            lows = [jnp.zeros((1, HDIM), F32)] * self.heads
            for ab, s, sp in self.units():
                q_ref, f_ref, v_ref = (qa_ref, qb_ref)[ab], (fa_ref, fb_ref)[ab], (va_ref, vb_ref)[ab]
                slot = sc[ab * n + p]
                valid = self.valid(sc, p, ab, s)
                queries, values = q_ref[0, 0, sp], v_ref[0, 0, sp]
                forget = f_ref[0, 0, sp]
                neg, keys, cum = self.rates(forget, lower_ref[...], valid)
                mid, last = cum[mid_row : mid_row + 1], cum[self.rows - 1 :]
                from_mid, to_mid = jnp.exp(cum - mid), jnp.exp(mid - cum)
                start_mid, mid_last = jnp.exp(mid), jnp.exp(last - mid)
                q_mid, k_mid = queries * from_mid, keys * to_mid
                q_start, k_last = q_mid * start_mid, k_mid * mid_last
                fade = jnp.exp(last)
                pos = jax.nn.sigmoid(forget)
                for h in range(self.heads):
                    at = self.state(ab, s, h)
                    ch = slice(h * HDIM, (h + 1) * HDIM)
                    gm, val = gm_ref[0, ab, sp, ch], values[:, ch]
                    start, back = start_ref[0, at] + fade_ref[0, at] * init_ref[at], back_ref[at]
                    scores = jnp.where(down, dot3(q_mid[:, ch], k_mid[:, ch], NT), 0.0)
                    pull = jnp.where(down, dot3(gm, val, NT), 0.0)
                    gq = from_mid[:, ch] * (
                        dot3(pull, k_mid[:, ch], NN) + dot3(gm, start, NN) * start_mid[:, ch]
                    )
                    gv = dot3(scores, gm, TN) + dot3(k_last[:, ch], back, NT)
                    gk = to_mid[:, ch] * (
                        dot3(pull, q_mid[:, ch], TN) + dot3(val, back, NN) * mid_last[:, ch]
                    )
                    at_end = jnp.sum(back * end_ref[at], axis=0, keepdims=True)
                    fading = at_end + summed(
                        up.astype(F32), queries[:, ch] * gq - keys[:, ch] * gk
                    )
                    gk = gk - fading / (1.0 - keys[:, ch])
                    gk_valid = gk * valid * neg[:, ch]
                    lows[h] += jnp.sum(gk_valid, axis=0, keepdims=True)
                    gf = -gk_valid * room[:, ch] * pos[:, ch]
                    for part, value in enumerate((gq, gf, gv)):
                        at_col = part * c + h * HDIM
                        out_ref[slot, ab, sp, at_col : at_col + HDIM] = value.astype(BF)
                    end_ref[at] = start
                    back_ref[at] = back * fade[:, ch] + dot3(gm, q_start[:, ch], TN)
            for h in range(self.heads):
                low_ref[:, h * HDIM : (h + 1) * HDIM] -= lows[h]

        shapes = [
            jax.ShapeDtypeStruct((n, 2, rows, 3 * c), BF),
            jax.ShapeDtypeStruct((1, c), F32),
        ]
        slots = lambda part: self.slots(part, c, True)
        states = self.whole((total, HDIM, HDIM))
        return self.call(
            kernel,
            slots(0) + slots(1) + slots(2)
            + [self.chunk(grad_mix.shape, True), self.chunk(starts.shape, True), self.chunk(fades.shape, True)]
            + [states] * 3
            + [self.whole((1, c))],
            [self.whole(x.shape) for x in shapes],
            shapes,
            [pltpu.VMEM((total, HDIM, HDIM), F32)] * 2,
            (joint,) * 6 + (grad_mix, starts, fades, initial, final, leaving, self.lower),
        )


def norm_back(values, gain, grad, epsilon):
    scale = lax.rsqrt(jnp.mean(values * values, axis=-1, keepdims=True) + epsilon)
    pulled = gain * grad
    grad_values = scale * pulled - values * (scale * scale * scale) * jnp.mean(
        values * pulled, axis=-1, keepdims=True
    )
    return grad_values, jnp.sum(values * scale * grad, axis=0)


def weight_grad(left, right):
    return lax.dot_general(left, right, TN, preferred_element_type=F32).astype(BF)


def shards(
    tokens,
    lengths,
    cotangent,
    mixer_gain,
    query_weight,
    forget_weight,
    input_weight,
    gate_weight,
    lower_bound,
    head_gain,
    out_weight,
    feed_gain,
    feed_gate_weight,
    up_weight,
    down_weight,
):
    count = lax.axis_size("hid")
    me = lax.axis_index("hid")
    rows, seqs, width = tokens.shape
    cols = query_weight.shape[1]
    units = feed_gate_weight.shape[1]
    base = lax.axis_index("seq") * (rows * count)
    own = seqs * rows
    cut = own // 2

    def halves_of(array):
        return array[:cut], array[cut:]

    def to_rows(array):
        return jnp.transpose(array, (1, 0, 2)).reshape(own, width)

    def from_rows(array):
        return jnp.transpose(array.reshape(seqs, rows, width), (1, 0, 2))

    flat = lambda x: x.reshape(-1, x.shape[-1])
    offsets = jnp.concatenate([jnp.arange(count), jnp.asarray(b_offsets(count))]) ^ me
    inverse = np.argsort(b_offsets(count)).astype(np.int32)
    places = jnp.arange(count) ^ me
    table = jnp.concatenate([places, jnp.asarray(inverse)[places]])
    scan = Scan(count, seqs, rows, cols, table, base, lengths, lower_bound)
    line = Line()
    gate_t, up_t = feed_gate_weight.T, up_weight.T

    own_rows = to_rows(tokens)
    inputs = own_rows.astype(F32)
    in_scale = lax.rsqrt(jnp.mean(inputs * inputs, axis=-1, keepdims=True) + 1e-06)
    normed_in = (inputs * in_scale * mixer_gain).astype(BF)
    going = Gather(*halves_of(normed_in))
    going.links(False)
    going.links(True)
    joint_weights = (query_weight, forget_weight, input_weight, gate_weight)
    joint_out = [(4 * cols, F32), (width, BF)]

    def project(group, place, before=None):
        def body(xs, w_refs):
            return [jnp.concatenate([dot(xs[0], w[...], NN) for w in w_refs], axis=1), xs[0]]

        return line(
            lambda group, before: stream(
                [group], place, count, joint_weights, joint_out, body, before
            ),
            group,
            before,
        )

    part = project(going.early(), None)
    cot_rows = tie(to_rows(cotangent), part[0])
    other = going.other((part[0], cot_rows))
    part = project(list(going.late), 0, part)
    cots = Gather(*tie(halves_of(cot_rows), other))
    cots.links(False)
    joint, in_rows = by_slot(project(other, 1, part))
    ends, fade, gate_sums = line(scan.ends, joint)
    entry = Entering(ends, fade, False)
    cots.links(True, (ends,))
    mixture, reach, starts, fades = line(scan.forward, joint)
    initial = entry.finish(line)
    mixture, gated_p = line(scan.finish, joint, mixture, reach, initial, head_gain)
    moved = lax.all_to_all(
        gated_p.reshape(count, own, cols), "hid", split_axis=0, concat_axis=0, tiled=True
    )
    cot_early = tie((cots.a, cots.b), gated_p)
    cot_early = list(cot_early) + [hop(x, 1) for x in cot_early]
    cot_other = cots.other((gated_p,))
    residual, normed_feed = line(
        lambda m, _: attend(m, out_weight, own_rows, feed_gain.reshape(1, width)),
        moved,
        (cot_early, cot_other),
    )

    going = Gather(*halves_of(normed_feed))
    going.links(False)
    going.links(True)
    feed_weights = (gate_t, up_t, down_weight)
    feed_shapes = [(units, BF)] * 3 + [(width, BF)] * 2

    def feed(group, cot_group, place, before=None):
        def body(xs, w_refs):
            gate = dot(xs[0], w_refs[0][...], NT)
            up = dot(xs[0], w_refs[1][...], NT)
            grad_hidden = dot(xs[1], w_refs[2][...], NT)
            sig = jax.nn.sigmoid(gate)
            silu = gate * sig
            grad_gate = grad_hidden * up * sig * (1.0 + gate * (1.0 - sig))
            return [silu * up, grad_gate, grad_hidden * silu, xs[0], xs[1]]

        return line(
            lambda group, cot_group, before: stream(
                [group, cot_group], place, count, feed_weights, feed_shapes, body, before
            ),
            group,
            cot_group,
            before,
        )

    part = feed(going.early(), cot_early, None)
    other = going.other((part[0],))
    part = feed(list(going.late), list(cots.late), 0, part)
    hidden, grad_feed_gate, grad_up, feed_rows, grad_rows = by_slot(
        feed(other, cot_other, 1, part)
    )
    hidden_f, gate_f, up_f = flat(hidden), flat(grad_feed_gate), flat(grad_up)
    feed_f, grad_f = flat(feed_rows), flat(grad_rows)
    sums = Sums()
    backs = lambda parity: line(
        lambda *a: partial_rows(a, (gate_t, up_t), NN, parity), grad_feed_gate, grad_up
    )
    shrink = Scatter(backs(1))
    even = backs(0)
    down_w = sums.push(line(weight_grad, hidden_f, grad_f))
    line(shrink.first, even)
    gate_w = line(weight_grad, gate_f, feed_f)
    while shrink.more():
        line(lambda *_: shrink.step())
    up_w = line(weight_grad, up_f, feed_f)

    def after_feed(grad):
        cot = to_rows(cotangent).astype(F32)
        grad_part, grad_gain = norm_back(residual, feed_gain, grad, 1e-06)
        grad_residual = cot + grad_part
        return grad_residual.astype(BF), grad_residual, grad_gain

    grad_attended, grad_residual, grad_feed_gain = line(after_feed, shrink.result())

    sent = line(lambda rows: head_rows(rows, out_weight, count), grad_attended)
    grad_gated = lax.all_to_all(sent, "hid", split_axis=0, concat_axis=0, tiled=True)
    sums.tick(line)
    gate_w = sums.push(gate_w)
    out_full = line(
        lambda m, g: lax.dot_general(
            m, g, (((1,), (0,)), ((), ())), preferred_element_type=F32
        ).astype(BF),
        moved,
        grad_attended,
    )
    grad_mix, grad_gate, grad_head, reach = line(
        scan.finish_back, joint, mixture, grad_gated.reshape(mixture.shape), head_gain
    )
    exit_ = Entering(reach, fade, True)
    in_f = flat(in_rows)
    mix_gate = line(weight_grad, in_f, flat(grad_gate))
    spread = lambda x: lax.psum_scatter(x, "hid", scatter_dimension=0, tiled=True)
    out_part = spread(tie(out_full.reshape(count * cols, width), mix_gate))
    leaving_done = exit_.take(line)
    feed_a, feed_b = line(owned_rows, hidden, down_weight, offsets)
    feed_out = jnp.concatenate([spread(feed_a), spread(feed_b)], axis=0)
    sums.tick(line)
    up_w = sums.push(up_w)
    leaving = exit_.border[0] if leaving_done else exit_.finish(line)
    final = ends + fade * initial
    grad_three, grad_lower = line(
        scan.backward, joint, grad_mix, starts, fades, initial, final, leaving
    )
    three_f = flat(grad_three)
    quarter = width // 4
    three = lambda i: line(
        lambda x, g: weight_grad(x[:, i * quarter : (i + 1) * quarter], g), in_f, three_f
    )
    threes = [three(0), three(1)]
    sums.tick(line)
    out_part = sums.push(out_part)
    joint_three = jnp.concatenate(joint_weights[:3], axis=1)
    backs = lambda parity: line(
        lambda *a: partial_rows(a, (joint_three, gate_weight), NT, parity), grad_three, grad_gate
    )
    shrink = Scatter(backs(1))
    threes += [three(2), three(3)]
    sums.tick(line)
    mix_gate = sums.push(mix_gate)
    even = backs(0)
    line(shrink.first, even)
    sums.tick(line)
    threes[0] = sums.push(threes[0])
    while shrink.more():
        line(lambda *_: shrink.step())
    sums.tick(line)
    threes[1] = sums.push(threes[1])
    grad_in, grad_mixer = line(lambda g: norm_back(inputs, mixer_gain, g, 1e-06), shrink.result())
    grad_tokens = line(lambda a, b: from_rows(a + b), grad_residual, grad_in)
    small = everywhere(
        jnp.concatenate([grad_mixer, grad_feed_gain, jnp.sum(gate_sums).reshape(1)]), "hid"
    )
    sums.tick(line)
    threes[2] = sums.push(threes[2])
    small = everywhere(jnp.concatenate([small, grad_lower[0], grad_head[0]]), "seq")
    heads = small[2 * width + 1 :]
    sums.tick(line)
    threes[3] = sums.push(threes[3])
    output = line(lambda a, b: from_rows((a + b).astype(BF)), residual, feed_out)
    gathered_out = lax.all_gather(out_part["total"], "hid", axis=0, tiled=True)
    sums.tick(line)
    grad_out = line(lambda x: x.astype(F32), gathered_out)
    sums.drain(line)
    total = lambda *parts: jnp.concatenate([p["total"] for p in parts], axis=0).astype(F32)
    three_w = total(*threes)
    mean_forget = small[2 * width] / (width * jnp.sum(lengths).astype(F32))
    return (
        output,
        grad_tokens,
        small[:width],
        three_w[:, :cols],
        three_w[:, cols : 2 * cols],
        three_w[:, 2 * cols :],
        total(mix_gate),
        heads[:cols],
        heads[cols:],
        grad_out,
        small[width : 2 * width],
        total(gate_w).T,
        total(up_w).T,
        total(down_w),
        mean_forget,
    )


def solution(mesh):
    rows = P(("seq", "hid"), None, None)
    columns = P(None, "hid")
    return jax.shard_map(
        shards,
        mesh=mesh,
        in_specs=(
            rows,
            P(),
            rows,
            P(),
            columns,
            columns,
            columns,
            columns,
            P("hid"),
            P("hid"),
            P(),
            P(),
            columns,
            columns,
            P("hid", None),
        ),
        out_specs=(
            rows,
            rows,
            P(),
            columns,
            columns,
            columns,
            columns,
            P("hid"),
            P("hid"),
            P(),
            P(),
            columns,
            columns,
            P("hid", None),
            P(),
        ),
        check_vma=False,
    )
```

time: 2230 us -> 975 us (0.44)
  waiting for transfers between devices: 1550 us -> 334 us
  Pallas kernels: 0 us -> 238 us
  matrix products: 276 us -> 61.5 us
  local copies, waits for them, and re-layouts: 174 us -> 27.1 us
  starting transfers between devices: 4.4 us -> 149 us
  blocking collectives: 83.5 us -> 19.6 us
    psum x2 -> x0, waiting for transfers between devices: 1100 us -> none  [the longest x1 862 us: shards(): lax.psum((grad_query_w, grad_forget_w, grad_input_w, grad_gate_w, grad_lo...]
    ppermute x0 -> x72, waiting for transfers between devices: none -> 334 us  [the longest x27 195 us: start(): lax.ppermute(value, 'seq', self.pairs[stage])]
    reduce_scatter x3, waiting for transfers between devices: 260 us -> 0.02 us  [shards(): lax.psum_scatter(x, 'hid', scatter_dimension=0, tiled=True)]
    pallas_call x0 -> x18, Pallas kernels: none -> 238 us  [the longest x5 95.5 us: call(): pl.pallas_call(kernel, grid_spec=pltpu.PrefetchScalarGridSpec(num_scalar_...]
    dot_general x28 -> x9, matrix products: 276 us -> 61.5 us  [the longest x8 55.7 us: weight_grad(): lax.dot_general(left, right, TN, preferred_element_type=F32).astype(BF)]
    all_gather x5 -> x1, waiting for transfers between devices: 165 us -> 0.01 us  [shards(): gathered_out = lax.all_gather(out_part['total'], 'hid', axis=0, tiled=True)]
    ppermute x0 -> x72, starting transfers between devices: none -> 145 us  [the longest x27 103 us: start(): lax.ppermute(value, 'seq', self.pairs[stage])]
    convert_element_type x5 -> x32, other arithmetic: 8.97 us -> 84.5 us  [the longest x18 47.8 us: turn(): (a.astype(F32) + b.astype(F32)).astype(BF)]
  transfers between devices with their start and end apart: 11 -> 77, of which waited for: 10 -> 35; matrix products, arithmetic and copies ran while one was open for 8% -> 18% of each run, Pallas kernels for 0% -> 20%
where the time goes in v1:
time: 975 us; the launch traced here: 962 us
  waiting for transfers between devices  334 us (34%)
  Pallas kernels  238 us (24%)
  starting transfers between devices  149 us (15%)
  other arithmetic  115 us (12%)
  matrix products  61.5 us (6%)
  local copies, waits for them, and re-layouts  27.1 us (3%)
  blocking collectives  19.6 us (2%)
  between operations  18.2 us (2%)
    ppermute x27, waiting for transfers between devices, start(): lax.ppermute(value, 'seq', self.pairs[stage])  195 us
    ppermute x34, waiting for transfers between devices, hop(): return lax.ppermute(array, 'hid', [(i, i ^ mask) for i in range(count)])  114 us
    ppermute x27, starting transfers between devices, start(): lax.ppermute(value, 'seq', self.pairs[stage])  103 us
    pallas_call x5, Pallas kernels, call(): pl.pallas_call(kernel, grid_spec=pltpu.PrefetchScalarGridSpec(num_scalar_...  95.5 us
    pallas_call x6, Pallas kernels, stream(): pl.pallas_call(kernel, grid=(steps,), in_specs=[anywhere] * n_arrays + [w...  72.5 us
    dot_general x8, matrix products, weight_grad(): lax.dot_general(left, right, TN, preferred_element_type=F32).astype(BF)  55.7 us
    convert_element_type x18, other arithmetic, turn(): (a.astype(F32) + b.astype(F32)).astype(BF)  47.8 us
    pallas_call x4, Pallas kernels, partial_rows(): pl.pallas_call(kernel, grid=(count // 2,), in_specs=[pl.BlockSpec((1, 2,...  39.9 us
  transfers between devices with their start and end apart: 77, of which 35 were waited for; matrix products, arithmetic and copies ran while one was open for 18% of the time, Pallas kernels for 20%

profile of v1, /device:TPU:0, one launch (start us, length us, event | category | flops | bytes accessed | tf_op | source)
XLA Modules:
  0.0 962.5 jit_solution(1350700419379247113)
XLA Ops:
  16.0 10.4 %collective-permute-done.2 = bf16[1,128,2048]{2,1,0:T(8,128)(2,1)S(1)} collective-permute-done((bf16[1,128,2048]{2,1,0:T(8,128)(2,1)S(1)}, bf16[1,128,2048]{2,1,0:T(8,128)(2,1)S(1)}, u32[]{:S(2)}, u32[]{:S(2)}) %collective-permute-start.2) | collective-permute-done | bytes 524320 | tf_op jit(solution)/shard_map/ppermute | solution.py:48
  32.1 9.8 %shard_map.280 = (f32[4,2,2,128,1024]{4,3,2,1,0:T(8,128)}, bf16[4,2,2,128,2048]{4,3,2,1,0:T(8,128)(2,1)}) custom-call(bf16[2,128,2048]{2,1,0:T(8,128)(2,1)} %copy-done.29, bf16[2,128,2048]{2,1,0:T(8,128)(2,1)} %copy-done.28, bf16[2,128,2048]{2,1,0:T(8,128)(2,1)} %collective-permute-done.4.refs_2_, bf16[2,128,2048]{2,1,0:T(8,128)(2,1)} %copy-done.48, ...), custom_call_target="tpu_custom_call" | custom-call | tf_op jit(solution)/shard_map/pallas_call | solution.py:289
  42.0 11.7 %collective-permute-done.3.refs_1_ = bf16[2,128,2048]{2,1,0:T(8,128)(2,1)} collective-permute-done((bf16[2,128,2048]{2,1,0:T(8,128)(2,1)S(1)}, bf16[2,128,2048]{2,1,0:T(8,128)(2,1)}, u32[]{:S(2)}, u32[]{:S(2)}) %collective-permute-start.3) | collective-permute-done | bytes 1048608 | tf_op jit(solution)/shard_map/ppermute | solution.py:48
  79.0 12.0 %shard_map.283 = (f32[8,128,128]{2,1,0:T(8,128)}, f32[8,1,128]{2,1,0:T(1,128)}, f32[1,256]{1,0:T(1,128)}) custom-call(s32[21]{0:T(128)} %pad_add_fusion.sc, f32[8,2,128,1024]{3,2,1,0:T(8,128)} %bitcast.146, f32[8,2,128,1024]{3,2,1,0:T(8,128)} %bitcast.147, f32[8,2,128,1024]{3,2,1,0:T(8,128)} %bitcast.148, f32[8,2,128,1024]{3,2,1,0:T(8,128)} %bitcast.149, ...), custom_call_target="tpu_custom_call" | custom-call | tf_op jit(solution)/shard_map/pallas_call | solution.py:462
  103.9 21.0 %shard_map.284 = (f32[8,2,128,256]{3,2,1,0:T(8,128)}, f32[8,2,128,256]{3,2,1,0:T(8,128)}, f32[8,8,128,128]{3,2,1,0:T(8,128)}, f32[8,8,1,128]{3,2,1,0:T(1,128)}) custom-call(s32[21]{0:T(128)} %pad_add_fusion.sc, f32[8,2,128,1024]{3,2,1,0:T(8,128)} %bitcast.150, f32[8,2,128,1024]{3,2,1,0:T(8,128)} %bitcast.151, f32[1,256]{1,0:T(1,128)} %bitcast.217), custom_call_target="tpu_custom_call" | custom-call | tf_op jit(solution)/shard_map/pallas_call | solution.py:462
  134.5 10.2 %shard_map.285 = (f32[8,2,128,256]{3,2,1,0:T(8,128)}, bf16[8,2,128,256]{3,2,1,0:T(8,128)(2,1)}) custom-call(s32[21]{0:T(128)} %pad_add_fusion.sc, f32[8,2,128,1024]{3,2,1,0:T(8,128)} %bitcast.152, f32[8,2,128,1024]{3,2,1,0:T(8,128)} %bitcast.153, f32[8,2,128,256]{3,2,1,0:T(8,128)} %get-tuple-element.264.local_ref, ...), custom_call_target="tpu_custom_call" | custom-call | tf_op jit(solution)/shard_map/pallas_call | solution.py:462
  145.9 19.6 %all_to_all.10.moved_ref = bf16[8,256,256]{2,1,0:T(8,128)(2,1)} all-to-all(bf16[8,256,256]{2,1,0:T(8,128)(2,1)} %bitcast.211), channel_id=1, replica_groups=mesh['seq'=4,'hid'=8] {'hid'}, dimensions={0} | all-to-all | bytes 2097152 | tf_op jit(solution)/shard_map/all_to_all | solution.py:872
  178.4 11.9 %collective-permute-done.21 = bf16[1,128,2048]{2,1,0:T(8,128)(2,1)S(1)} collective-permute-done((bf16[1,128,2048]{2,1,0:T(8,128)(2,1)S(1)}, bf16[1,128,2048]{2,1,0:T(8,128)(2,1)S(1)}, u32[]{:S(2)}, u32[]{:S(2)}) %collective-permute-start.21) | collective-permute-done | bytes 524320 | tf_op jit(solution)/shard_map/ppermute | solution.py:48
  195.6 18.3 %shard_map.287 = (bf16[4,2,2,128,704]{4,3,2,1,0:T(8,128)(2,1)}, bf16[4,2,2,128,704]{4,3,2,1,0:T(8,128)(2,1)}, bf16[4,2,2,128,704]{4,3,2,1,0:T(8,128)(2,1)}, bf16...) custom-call(bf16[2,128,2048]{2,1,0:T(8,128)(2,1)} %copy-done.25, bf16[2,128,2048]{2,1,0:T(8,128)(2,1)} %copy-done.24, ...), custom_call_target="tpu_custom_call" | custom-call | tf_op jit(solution)/shard_map/pallas_call | solution.py:289
  217.9 14.0 %shard_map.288 = (bf16[4,2,2,128,704]{4,3,2,1,0:T(8,128)(2,1)}, bf16[4,2,2,128,704]{4,3,2,1,0:T(8,128)(2,1)}, bf16[4,2,2,128,704]{4,3,2,1,0:T(8,128)(2,1)}, bf16...) custom-call(bf16[2,128,2048]{2,1,0:T(8,128)(2,1)} %collective-permut, ...), custom_call_target="tpu_custom_call", output_to_operand_aliasing={{0}: (7, {}), {1}: (8, {}), {2}: (9, {}), {3}: (10, {}), {4... | custom-call | tf_op jit(solution)/shard_map/pallas_call | solution.py:289
  233.2 14.1 %shard_map.289 = (bf16[4,2,2,128,704]{4,3,2,1,0:T(8,128)(2,1)}, bf16[4,2,2,128,704]{4,3,2,1,0:T(8,128)(2,1)}, bf16[4,2,2,128,704]{4,3,2,1,0:T(8,128)(2,1)}, bf16...) custom-call(bf16[2,128,2048]{2,1,0:T(8,128)(2,1)} %copy-done.43, ...), custom_call_target="tpu_custom_call", output_to_operand_aliasing={{0}: (7, {}), {1}: (8, {}), {2}: (9, {}), {3}: (10, {}), {4... | custom-call | tf_op jit(solution)/shard_map/pallas_call | solution.py:289
  247.3 11.2 %shard_map.290 = bf16[2,4,128,2048]{3,2,1,0:T(8,128)(2,1)} custom-call(bf16[8,2,128,704]{3,2,1,0:T(8,128)(2,1)} %bitcast.176, bf16[8,2,128,704]{3,2,1,0:T(8,128)(2,1)} %bitcast.179, bf16[704,2048]{1,0:T(8,128)(2,1)} %bitcast.169, bf16[704,2048]{1,0:T(8,128)(2,1)} %bitcast.174), custom_call_target="tpu_custom_call" | custom-call | tf_op jit(solution)/shard_map/pallas_call | solution.py:340
  258.5 11.3 %shard_map.291 = bf16[2,4,128,2048]{3,2,1,0:T(8,128)(2,1)} custom-call(bf16[8,2,128,704]{3,2,1,0:T(8,128)(2,1)} %bitcast.177, bf16[8,2,128,704]{3,2,1,0:T(8,128)(2,1)} %bitcast.180, bf16[704,2048]{1,0:T(8,128)(2,1)} %bitcast.170, bf16[704,2048]{1,0:T(8,128)(2,1)} %bitcast.175), custom_call_target="tpu_custom_call" | custom-call | tf_op jit(solution)/shard_map/pallas_call | solution.py:340
  269.8 10.1 %convolution_convert_fusion.3 = bf16[704,2048]{1,0:T(8,128)(2,1)} fusion(bf16[2048,704]{1,0:T(8,128)(2,1)S(1)} %bitcast.192, bf16[2048,2048]{1,0:T(8,128)(2,1)} %bitcast.184), kind=kOutput, calls=%fused_computation.12 | convolution fusion | flops 5907021824 | bytes 14155776 | tf_op jit(solution)/shard_map/dot_general | solution.py:790
  293.9 14.2 %collective-permute-done.28 = bf16[2,128,2048]{2,1,0:T(8,128)(2,1)S(1)} collective-permute-done((bf16[2,128,2048]{2,1,0:T(8,128)(2,1)S(1)}, bf16[2,128,2048]{2,1,0:T(8,128)(2,1)S(1)}, u32[]{:S(2)}, u32[]{:S(2)}) %collective-permute-start.28) | collective-permute-done | bytes 1048608 | tf_op jit(solution)/shard_map/ppermute | solution.py:48
  343.2 11.5 %collective-permute-done.32 = bf16[704,2048]{1,0:T(8,128)(2,1)} collective-permute-done((bf16[704,2048]{1,0:T(8,128)(2,1)}, bf16[704,2048]{1,0:T(8,128)(2,1)}, u32[]{:S(2)}, u32[]{:S(2)}) %collective-permute-start.32) | collective-permute-done | bytes 2883616 | tf_op jit(solution)/shard_map/ppermute | solution.py:137
  367.1 12.6 %shard_map.293 = (f32[8,2,128,256]{3,2,1,0:T(8,128)}, bf16[8,2,128,256]{3,2,1,0:T(8,128)(2,1)}, f32[1,256]{1,0:T(1,128)}, f32[8,128,128]{2,1,0:T(8,128)}) custom-call(s32[21]{0:T(128)} %pad_add_fusion.sc, f32[8,2,128,1024]{3,2,1,0:T(8,128)} %bitcast.154, f32[8,2,128,1024]{3,2,1,0:T(8,128)} %bitcast.155, f32[8,2,128,1024]{3,2,1,0:T(8,128)} %bitcast.156, ...), custom_call_target="tpu_custom_call" | custom-call | tf_op jit(solution)/shard_map/pallas_call | solution.py:462
  388.9 9.8 %convolution_convert_fusion.1 = bf16[704,2048]{1,0:T(8,128)(2,1)} fusion(bf16[2048,704]{1,0:T(8,128)(2,1)S(1)} %bitcast.178, bf16[2048,2048]{1,0:T(8,128)(2,1)} %bitcast.183), kind=kOutput, calls=%fused_computation.10 | convolution fusion | flops 5907021824 | bytes 14155776 | tf_op jit(solution)/shard_map/dot_general | solution.py:790
  416.5 12.8 %shard_map.294 = (bf16[1024,2048]{1,0:T(8,128)(2,1)}, bf16[1024,2048]{1,0:T(8,128)(2,1)}) custom-call(s32[16]{0:T(128)} %broadcast_xor_fusion._, bf16[8,2,128,704]{3,2,1,0:T(8,128)(2,1)} %bitcast.191, bf16[704,2048]{1,0:T(8,128)(2,1)} %weight_ref.4), custom_call_target="tpu_custom_call" | custom-call | tf_op jit(solution)/shard_map/pallas_call | solution.py:363
  433.3 31.3 %collective-permute-done.37 = bf16[704,2048]{1,0:T(8,128)(2,1)} collective-permute-done((bf16[704,2048]{1,0:T(8,128)(2,1)}, bf16[704,2048]{1,0:T(8,128)(2,1)}, u32[]{:S(2)}, u32[]{:S(2)}) %collective-permute-start.37) | collective-permute-done | bytes 2883616 | tf_op jit(solution)/shard_map/ppermute | solution.py:137
  464.6 30.0 %collective-permute-start.38 = (bf16[704,2048]{1,0:T(8,128)(2,1)}, bf16[704,2048]{1,0:T(8,128)(2,1)}, u32[]{:S(2)}, u32[]{:S(2)}) collective-permute-start(bf16[704,2048]{1,0:T(8,128)(2,1)} %convolution_convert_fusion.2), channel_id=1, source_target_pairs={{0,8},{24,16},{1,9},{25,17},{2,10},{26,18},{3,11},{27,19},{4,12},{... | collective-permute-start | bytes 8650760 | tf_op jit(solution)/shard_map/ppermute | solution.py:137
  511.5 39.8 %shard_map.295 = (bf16[8,2,128,768]{3,2,1,0:T(8,128)(2,1)}, f32[1,256]{1,0:T(1,128)}) custom-call(s32[21]{0:T(128)} %pad_add_fusion.sc, f32[8,2,128,1024]{3,2,1,0:T(8,128)} %bitcast.160, f32[8,2,128,1024]{3,2,1,0:T(8,128)} %bitcast.161, f32[8,2,128,1024]{3,2,1,0:T(8,128)} %bitcast.162, f32[8,2,128,1024]{3,2,1,0:T(8,128)} %bitcast.163, ...), custom_call_target="tpu_custom_call" | custom-call | tf_op jit(solution)/shard_map/pallas_call | solution.py:462
  603.0 14.0 %collective-permute-done.39 = bf16[256,2048]{1,0:T(8,128)(2,1)S(1)} collective-permute-done((bf16[256,2048]{1,0:T(8,128)(2,1)}, bf16[256,2048]{1,0:T(8,128)(2,1)S(1)}, u32[]{:S(2)}, u32[]{:S(2)}) %collective-permute-start.39) | collective-permute-done | bytes 1048608 | tf_op jit(solution)/shard_map/ppermute | solution.py:137
  621.6 32.0 %collective-permute-done.61 = bf16[704,2048]{1,0:T(8,128)(2,1)} collective-permute-done((bf16[704,2048]{1,0:T(8,128)(2,1)}, bf16[704,2048]{1,0:T(8,128)(2,1)}, u32[]{:S(2)}, u32[]{:S(2)}) %collective-permute-start.61) | collective-permute-done | bytes 2883616 | tf_op jit(solution)/shard_map/ppermute | solution.py:137
  688.6 31.0 %collective-permute-done.62 = bf16[704,2048]{1,0:T(8,128)(2,1)} collective-permute-done((bf16[704,2048]{1,0:T(8,128)(2,1)S(1)}, bf16[704,2048]{1,0:T(8,128)(2,1)}, u32[]{:S(2)}, u32[]{:S(2)}) %collective-permute-start.62) | collective-permute-done | bytes 2883616 | tf_op jit(solution)/shard_map/ppermute | solution.py:137
  720.9 24.7 %collective-permute-done.63 = bf16[256,2048]{1,0:T(8,128)(2,1)S(1)} collective-permute-done((bf16[256,2048]{1,0:T(8,128)(2,1)}, bf16[256,2048]{1,0:T(8,128)(2,1)S(1)}, u32[]{:S(2)}, u32[]{:S(2)}) %collective-permute-start.63) | collective-permute-done | bytes 1048608 | tf_op jit(solution)/shard_map/ppermute | solution.py:137
  748.4 32.9 %collective-permute-done.46 = bf16[2,128,2048]{2,1,0:T(8,128)(2,1)S(1)} collective-permute-done((bf16[2,128,2048]{2,1,0:T(8,128)(2,1)}, bf16[2,128,2048]{2,1,0:T(8,128)(2,1)S(1)}, u32[]{:S(2)}, u32[]{:S(2)}) %collective-permute-start.46) | collective-permute-done | bytes 1048608 | tf_op jit(solution)/shard_map/ppermute | solution.py:48
  792.5 16.4 %collective-permute-done.47 = bf16[1,128,2048]{2,1,0:T(8,128)(2,1)S(1)} collective-permute-done((bf16[1,128,2048]{2,1,0:T(8,128)(2,1)}, bf16[1,128,2048]{2,1,0:T(8,128)(2,1)S(1)}, u32[]{:S(2)}, u32[]{:S(2)}) %collective-permute-start.47) | collective-permute-done | bytes 524320 | tf_op jit(solution)/shard_map/ppermute | solution.py:48
  839.4 14.3 %collective-permute-done.58 = f32[4609]{0:T(1024)S(1)} collective-permute-done((f32[4609]{0:T(1024)S(1)}, f32[4609]{0:T(1024)S(1)}, u32[]{:S(2)}, u32[]{:S(2)}) %collective-permute-start.58) | collective-permute-done | bytes 18468 | tf_op jit(solution)/shard_map/ppermute | solution.py:189
  905.3 11.3 %collective-permute-done.66 = bf16[512,768]{1,0:T(8,128)(2,1)S(1)} collective-permute-done((bf16[512,768]{1,0:T(8,128)(2,1)S(1)}, bf16[512,768]{1,0:T(8,128)(2,1)S(1)}, u32[]{:S(2)}, u32[]{:S(2)}) %collective-permute-start.66) | collective-permute-done | bytes 786464 | tf_op jit(solution)/shard_map/ppermute | solution.py:137
  920.9 11.7 %convert_element_type.638 = f32[2048,2048]{1,0:T(8,128)} convert(bf16[2048,2048]{1,0:T(8,128)(2,1)} %all-gather.2.cloned.1.call-done) | non-fusion elementwise | flops 4194304 | bytes 25165824 | tf_op jit(solution)/shard_map/convert_element_type | solution.py:1005
  936.8 14.1 %collective-permute-done.71 = bf16[512,768]{1,0:T(8,128)(2,1)S(1)} collective-permute-done((bf16[512,768]{1,0:T(8,128)(2,1)S(1)}, bf16[512,768]{1,0:T(8,128)(2,1)S(1)}, u32[]{:S(2)}, u32[]{:S(2)}) %collective-permute-start.71) | collective-permute-done | bytes 786464 | tf_op jit(solution)/shard_map/ppermute | solution.py:137
  (381 shorter events, 394.1 us)
Async XLA Ops:
  28.1 25.7 %collective-permute-start.3 = (bf16[2,128,2048]{2,1,0:T(8,128)(2,1)S(1)}, bf16[2,128,2048]{2,1,0:T(8,128)(2,1)}, u32[]{:S(2)}, u32[]{:S(2)}) collective-permute-start(bf16[2,128,2048]{2,1,0:T(8,128)(2,1)S(1)} %pad_maximum_fusion.3.refs_1_), channel_id=1, source_target_pairs={{0,2},{1,3},{2,0},{3,1},{4,6},{5,7},{6,4},{7,5},{8,10},{9,11},{10,... | collective-permute-start | bytes 3145736 | tf_op jit(solution)/shard_map/ppermute | solution.py:48
  60.3 36.0 %collective-permute-start.12 = (bf16[1,128,2048]{2,1,0:T(8,128)(2,1)S(1)}, bf16[1,128,2048]{2,1,0:T(8,128)(2,1)S(1)}, u32[]{:S(2)}, u32[]{:S(2)}) collective-permute-start(bf16[1,128,2048]{2,1,0:T(8,128)(2,1)S(1)} %bitcast.207), channel_id=1, source_target_pairs={{0,4},{1,5},{2,6},{3,7},{4,0},{5,1},{6,2},{7,3},{8,12},{9,13},{10,... | collective-permute-start | bytes 1572872 | tf_op jit(solution)/shard_map/ppermute | solution.py:48
  60.8 35.5 %collective-permute-start.11 = (bf16[1,128,2048]{2,1,0:T(8,128)(2,1)S(1)}, bf16[1,128,2048]{2,1,0:T(8,128)(2,1)}, u32[]{:S(2)}, u32[]{:S(2)}) collective-permute-start(bf16[1,128,2048]{2,1,0:T(8,128)(2,1)S(1)} %bitcast.205), channel_id=1, source_target_pairs={{0,2},{1,3},{2,0},{3,1},{4,6},{5,7},{6,4},{7,5},{8,10},{9,11},{10,... | collective-permute-start | bytes 1572872 | tf_op jit(solution)/shard_map/ppermute | solution.py:48
  92.1 32.8 %collective-permute-start.8 = (bf16[8,128,128]{2,1,0:T(8,128)(2,1)S(1)}, bf16[8,128,128]{2,1,0:T(8,128)(2,1)}, u32[]{:S(2)}, u32[]{:S(2)}) collective-permute-start(bf16[8,128,128]{2,1,0:T(8,128)(2,1)S(1)} %convert_element_type.510), channel_id=1, source_target_pairs={{0,8},{8,16},{16,24},{1,9},{9,17},{17,25},{2,10},{10,18},{18,26},{... | collective-permute-start | bytes 786440 | tf_op jit(solution)/shard_map/ppermute | solution.py:206
  97.9 47.4 %collective-permute-start.15 = (bf16[2,128,2048]{2,1,0:T(8,128)(2,1)S(1)}, bf16[2,128,2048]{2,1,0:T(8,128)(2,1)S(1)}, u32[]{:S(2)}, u32[]{:S(2)}) collective-permute-start(bf16[2,128,2048]{2,1,0:T(8,128)(2,1)S(1)} %pad_maximum_fusion.4.refs_4_), channel_id=1, source_target_pairs={{0,4},{1,5},{2,6},{3,7},{4,0},{5,1},{6,2},{7,3},{8,12},{9,13},{10,... | collective-permute-start | bytes 3145736 | tf_op jit(solution)/shard_map/ppermute | solution.py:48
  99.5 45.8 %collective-permute-start.16 = (bf16[2,128,2048]{2,1,0:T(8,128)(2,1)S(1)}, bf16[2,128,2048]{2,1,0:T(8,128)(2,1)}, u32[]{:S(2)}, u32[]{:S(2)}) collective-permute-start(bf16[2,128,2048]{2,1,0:T(8,128)(2,1)S(1)} %pad_maximum_fusion.5.refs_5_), channel_id=1, source_target_pairs={{0,2},{1,3},{2,0},{3,1},{4,6},{5,7},{6,4},{7,5},{8,10},{9,11},{10,... | collective-permute-start | bytes 3145736 | tf_op jit(solution)/shard_map/ppermute | solution.py:48
  282.4 25.7 %collective-permute-start.28 = (bf16[2,128,2048]{2,1,0:T(8,128)(2,1)S(1)}, bf16[2,128,2048]{2,1,0:T(8,128)(2,1)S(1)}, u32[]{:S(2)}, u32[]{:S(2)}) collective-permute-start(bf16[2,128,2048]{2,1,0:T(8,128)(2,1)S(1)} %get-tuple-element.471), channel_id=1, source_target_pairs={{0,4},{1,5},{2,6},{3,7},{4,0},{5,1},{6,2},{7,3},{8,12},{9,13},{10,... | collective-permute-start | bytes 3145736 | tf_op jit(solution)/shard_map/ppermute | solution.py:48
  284.9 69.8 %collective-permute-start.32 = (bf16[704,2048]{1,0:T(8,128)(2,1)}, bf16[704,2048]{1,0:T(8,128)(2,1)}, u32[]{:S(2)}, u32[]{:S(2)}) collective-permute-start(bf16[704,2048]{1,0:T(8,128)(2,1)} %convolution_convert_fusion.3), channel_id=1, source_target_pairs={{0,8},{24,16},{1,9},{25,17},{2,10},{26,18},{3,11},{27,19},{4,12},{... | collective-permute-start | bytes 8650760 | tf_op jit(solution)/shard_map/ppermute | solution.py:137
  339.3 26.8 %all-to-all-start.1 = ((bf16[8,256,256]{2,1,0:T(8,128)(2,1)}), bf16[8,256,256]{2,1,0:T(8,128)(2,1)S(1)}, u32[]{:S(2)}, u32[]{:S(2)}) async-start(bf16[8,256,256]{2,1,0:T(8,128)(2,1)} %shard_map.292), calls=%async_computation.1 | async-start | bytes 2097152 | tf_op jit(solution)/shard_map/all_to_all | solution.py:939
  342.9 242.2 %reduce-scatter.8.cloned.1.call-start = ((), (), s32[]{:S(2)}) async-start(), calls=%async_computation.7 | async-start | bytes 9437184 | tf_op jit(solution)/shard_map/reduce_scatter | solution.py:955
  387.0 438.0 %reduce-scatter.4.cloned.1.call-start = ((), (), s32[]{:S(2)}) async-start(), calls=%async_computation.5 | async-start | bytes 4718592 | tf_op jit(solution)/shard_map/reduce_scatter | solution.py:955
  398.7 65.9 %collective-permute-start.37 = (bf16[704,2048]{1,0:T(8,128)(2,1)}, bf16[704,2048]{1,0:T(8,128)(2,1)}, u32[]{:S(2)}, u32[]{:S(2)}) collective-permute-start(bf16[704,2048]{1,0:T(8,128)(2,1)} %convolution_convert_fusion.1), channel_id=1, source_target_pairs={{0,8},{24,16},{1,9},{25,17},{2,10},{26,18},{3,11},{27,19},{4,12},{... | collective-permute-start | bytes 8650760 | tf_op jit(solution)/shard_map/ppermute | solution.py:137
  404.8 96.0 %collective-permute-start.36 = (bf16[704,2048]{1,0:T(8,128)(2,1)}, bf16[704,2048]{1,0:T(8,128)(2,1)}, u32[]{:S(2)}, u32[]{:S(2)}) collective-permute-start(bf16[704,2048]{1,0:T(8,128)(2,1)} %add_convert_fusion.5), channel_id=1, source_target_pairs={{8,16},{16,8},{9,17},{17,9},{10,18},{18,10},{11,19},{19,11},{12,20... | collective-permute-start | bytes 8650760 | tf_op jit(solution)/shard_map/ppermute | solution.py:137
  429.3 395.7 %reduce-scatter.6.cloned.1.call-start = ((), (), s32[]{:S(2)}) async-start(), calls=%async_computation.6 | async-start | bytes 4718592 | tf_op jit(solution)/shard_map/reduce_scatter | solution.py:955
  432.0 78.5 %collective-permute-start.35 = (bf16[8,128,128]{2,1,0:T(8,128)(2,1)S(1)}, bf16[8,128,128]{2,1,0:T(8,128)(2,1)S(1)}, u32[]{:S(2)}, u32[]{:S(2)}) collective-permute-start(bf16[8,128,128]{2,1,0:T(8,128)(2,1)S(1)} %get-tuple-element.482), channel_id=1, source_target_pairs={{16,0},{24,8},{17,1},{25,9},{18,2},{26,10},{19,3},{27,11},{20,4},{... | collective-permute-start | bytes 786440 | tf_op jit(solution)/shard_map/ppermute | solution.py:206
  464.6 96.5 %collective-permute-start.38 = (bf16[704,2048]{1,0:T(8,128)(2,1)}, bf16[704,2048]{1,0:T(8,128)(2,1)}, u32[]{:S(2)}, u32[]{:S(2)}) collective-permute-start(bf16[704,2048]{1,0:T(8,128)(2,1)} %convolution_convert_fusion.2), channel_id=1, source_target_pairs={{0,8},{24,16},{1,9},{25,17},{2,10},{26,18},{3,11},{27,19},{4,12},{... | collective-permute-start | bytes 8650760 | tf_op jit(solution)/shard_map/ppermute | solution.py:137
  500.7 66.1 %collective-permute-start.43 = (bf16[704,2048]{1,0:T(8,128)(2,1)}, bf16[704,2048]{1,0:T(8,128)(2,1)}, u32[]{:S(2)}, u32[]{:S(2)}) collective-permute-start(bf16[704,2048]{1,0:T(8,128)(2,1)} %add_convert_fusion.4), channel_id=1, source_target_pairs={{8,16},{16,8},{9,17},{17,9},{10,18},{18,10},{11,19},{19,11},{12,20... | collective-permute-start | bytes 8650760 | tf_op jit(solution)/shard_map/ppermute | solution.py:137
  509.2 74.3 %collective-permute-start.60 = (bf16[704,2048]{1,0:T(8,128)(2,1)}, bf16[704,2048]{1,0:T(8,128)(2,1)}, u32[]{:S(2)}, u32[]{:S(2)}) collective-permute-start(bf16[704,2048]{1,0:T(8,128)(2,1)} %add_convert_fusion.3), channel_id=1, source_target_pairs={{8,0},{16,24},{9,1},{17,25},{10,2},{18,26},{11,3},{19,27},{12,4},{... | collective-permute-start | bytes 8650760 | tf_op jit(solution)/shard_map/ppermute | solution.py:137
  566.8 50.7 %collective-permute-start.44 = (bf16[704,2048]{1,0:T(8,128)(2,1)}, bf16[704,2048]{1,0:T(8,128)(2,1)}, u32[]{:S(2)}, u32[]{:S(2)}) collective-permute-start(bf16[704,2048]{1,0:T(8,128)(2,1)} %add_convert_fusion.2), channel_id=1, source_target_pairs={{8,16},{16,8},{9,17},{17,9},{10,18},{18,10},{11,19},{19,11},{12,20... | collective-permute-start | bytes 8650760 | tf_op jit(solution)/shard_map/ppermute | solution.py:137
  583.5 88.7 %collective-permute-start.45 = (bf16[2,4,128,2048]{3,2,1,0:T(8,128)(2,1)}, bf16[2,4,128,2048]{3,2,1,0:T(8,128)(2,1)}, u32[]{:S(2)}, u32[]{:S(2)}) collective-permute-start(bf16[2,4,128,2048]{3,2,1,0:T(8,128)(2,1)} %shard_map.296), channel_id=1, source_target_pairs={{0,1},{1,0},{2,3},{3,2},{4,5},{5,4},{6,7},{7,6},{8,9},{9,8},{10,11... | collective-permute-start | bytes 12582920 | tf_op jit(solution)/shard_map/ppermute | solution.py:48
  583.5 70.0 %collective-permute-start.61 = (bf16[704,2048]{1,0:T(8,128)(2,1)}, bf16[704,2048]{1,0:T(8,128)(2,1)}, u32[]{:S(2)}, u32[]{:S(2)}) collective-permute-start(bf16[704,2048]{1,0:T(8,128)(2,1)} %add_convert_fusion.1), channel_id=1, source_target_pairs={{8,0},{16,24},{9,1},{17,25},{10,2},{18,26},{11,3},{19,27},{12,4},{... | collective-permute-start | bytes 8650760 | tf_op jit(solution)/shard_map/ppermute | solution.py:137
  585.1 335.8 %all-gather.2.cloned.1.call-start = ((), (), s32[]{:S(2)}) async-start(), calls=%async_computation.8 | async-start | bytes 9437184 | tf_op jit(solution)/shard_map/all_gather | solution.py:1003
  585.2 31.9 %collective-permute-start.39 = (bf16[256,2048]{1,0:T(8,128)(2,1)}, bf16[256,2048]{1,0:T(8,128)(2,1)S(1)}, u32[]{:S(2)}, u32[]{:S(2)}) collective-permute-start(bf16[256,2048]{1,0:T(8,128)(2,1)} %reduce-scatter.8.cloned.1.call-done), channel_id=1, source_target_pairs={{0,8},{24,16},{1,9},{25,17},{2,10},{26,18},{3,11},{27,19},{4,12},{... | collective-permute-start | bytes 3145736 | tf_op jit(solution)/shard_map/ppermute | solution.py:137
  653.5 66.1 %collective-permute-start.62 = (bf16[704,2048]{1,0:T(8,128)(2,1)S(1)}, bf16[704,2048]{1,0:T(8,128)(2,1)}, u32[]{:S(2)}, u32[]{:S(2)}) collective-permute-start(bf16[704,2048]{1,0:T(8,128)(2,1)S(1)} %add_convert_fusion), channel_id=1, source_target_pairs={{8,0},{16,24},{9,1},{17,25},{10,2},{18,26},{11,3},{19,27},{12,4},{... | collective-permute-start | bytes 8650760 | tf_op jit(solution)/shard_map/ppermute | solution.py:137
  654.8 28.4 %collective-permute-start.40 = (bf16[2048,256]{1,0:T(8,128)(2,1)}, bf16[2048,256]{1,0:T(8,128)(2,1)}, u32[]{:S(2)}, u32[]{:S(2)}) collective-permute-start(bf16[2048,256]{1,0:T(8,128)(2,1)} %convolution_convert_fusion.4), channel_id=1, source_target_pairs={{0,8},{24,16},{1,9},{25,17},{2,10},{26,18},{3,11},{27,19},{4,12},{... | collective-permute-start | bytes 3145736 | tf_op jit(solution)/shard_map/ppermute | solution.py:137
  719.6 26.0 %collective-permute-start.63 = (bf16[256,2048]{1,0:T(8,128)(2,1)}, bf16[256,2048]{1,0:T(8,128)(2,1)S(1)}, u32[]{:S(2)}, u32[]{:S(2)}) collective-permute-start(bf16[256,2048]{1,0:T(8,128)(2,1)} %add_convert_fusion.6), channel_id=1, source_target_pairs={{8,0},{16,24},{9,1},{17,25},{10,2},{18,26},{11,3},{19,27},{12,4},{... | collective-permute-start | bytes 3145736 | tf_op jit(solution)/shard_map/ppermute | solution.py:137
  746.7 34.5 %collective-permute-start.46 = (bf16[2,128,2048]{2,1,0:T(8,128)(2,1)}, bf16[2,128,2048]{2,1,0:T(8,128)(2,1)S(1)}, u32[]{:S(2)}, u32[]{:S(2)}) collective-permute-start(bf16[2,128,2048]{2,1,0:T(8,128)(2,1)} %get-tuple-element.465), channel_id=1, source_target_pairs={{0,4},{1,5},{2,6},{3,7},{4,0},{5,1},{6,2},{7,3},{8,12},{9,13},{10,... | collective-permute-start | bytes 3145736 | tf_op jit(solution)/shard_map/ppermute | solution.py:48
  747.4 33.9 %collective-permute-start.48 = (bf16[2,128,2048]{2,1,0:T(8,128)(2,1)S(1)}, bf16[2,128,2048]{2,1,0:T(8,128)(2,1)S(1)}, u32[]{:S(2)}, u32[]{:S(2)}) collective-permute-start(bf16[2,128,2048]{2,1,0:T(8,128)(2,1)S(1)} %copy-done.47), channel_id=1, source_target_pairs={{0,2},{1,3},{2,0},{3,1},{4,6},{5,7},{6,4},{7,5},{8,10},{9,11},{10,... | collective-permute-start | bytes 3145736 | tf_op jit(solution)/shard_map/ppermute | solution.py:48
  833.9 28.2 %collective-permute-start.42 = (bf16[512,768]{1,0:T(8,128)(2,1)}, bf16[512,768]{1,0:T(8,128)(2,1)}, u32[]{:S(2)}, u32[]{:S(2)}) collective-permute-start(bf16[512,768]{1,0:T(8,128)(2,1)} %fusion.18), channel_id=1, source_target_pairs={{0,8},{24,16},{1,9},{25,17},{2,10},{26,18},{3,11},{27,19},{4,12},{... | collective-permute-start | bytes 2359304 | tf_op jit(solution)/shard_map/ppermute | solution.py:137
  837.7 31.5 %collective-permute-start.52 = (bf16[512,768]{1,0:T(8,128)(2,1)}, bf16[512,768]{1,0:T(8,128)(2,1)}, u32[]{:S(2)}, u32[]{:S(2)}) collective-permute-start(bf16[512,768]{1,0:T(8,128)(2,1)} %add_convert_fusion.22), channel_id=1, source_target_pairs={{8,16},{16,8},{9,17},{17,9},{10,18},{18,10},{11,19},{19,11},{12,20... | collective-permute-start | bytes 2359304 | tf_op jit(solution)/shard_map/ppermute | solution.py:137
  854.6 25.6 %collective-permute-start.64 = (bf16[2048,256]{1,0:T(8,128)(2,1)}, bf16[2048,256]{1,0:T(8,128)(2,1)}, u32[]{:S(2)}, u32[]{:S(2)}) collective-permute-start(bf16[2048,256]{1,0:T(8,128)(2,1)} %add_convert_fusion.8), channel_id=1, source_target_pairs={{8,0},{16,24},{9,1},{17,25},{10,2},{18,26},{11,3},{19,27},{12,4},{... | collective-permute-start | bytes 3145736 | tf_op jit(solution)/shard_map/ppermute | solution.py:137
  903.5 29.1 %collective-permute-start.70 = (bf16[512,768]{1,0:T(8,128)(2,1)S(1)}, bf16[512,768]{1,0:T(8,128)(2,1)}, u32[]{:S(2)}, u32[]{:S(2)}) collective-permute-start(bf16[512,768]{1,0:T(8,128)(2,1)S(1)} %add_convert_fusion.17), channel_id=1, source_target_pairs={{8,16},{16,8},{9,17},{17,9},{10,18},{18,10},{11,19},{19,11},{12,20... | collective-permute-start | bytes 2359304 | tf_op jit(solution)/shard_map/ppermute | solution.py:137
  (111 other events, 1650.6 us)
Sparse Core Ops, SparseCore 0:
  387.1 71.1 reduce-scatter.7
  462.6 71.9 reduce-scatter.3
  585.2 54.3 reduce-scatter.5
  746.9 73.4 all-gather.1

commit v2 on v1

--- a/solution.py
+++ b/solution.py
@@ -82,9 +82,9 @@
     def early(self):
         return [self.a, self.b, hop(self.a, 1), hop(self.b, 1)]
 
-    def other(self, after=()):
+    def latest(self, after=()):
         sent = tie(self.late, *after) if after else self.late
-        return [hop(x, 1) for x in sent]
+        return list(self.late) + [hop(x, 1) for x in sent]
 
 
 class Scatter:
@@ -172,13 +172,14 @@
 
 class Line:
     def __init__(self):
-        self.token = None
+        self.before = ()
 
     def __call__(self, function, *args):
-        if self.token is not None:
-            args = tie(args, self.token)
+        if self.before and args:
+            args = tie(args, *self.before)
         result = function(*args)
-        self.token = jax.tree.leaves(result)[0]
+        leaf = jax.tree.leaves(result)[0]
+        self.before = (leaf,) if args else self.before + (leaf,)
         return result
 
 
@@ -193,52 +194,26 @@
 
 class Entering:
     def __init__(self, state, fade, reverse):
-        self.count = lax.axis_size("seq")
-        self.reverse = reverse
-        self.reach, self.cover, self.fade = 1, state, fade
-        self.border = None
-        self.send()
-
-    def send(self):
-        step = -self.reach if self.reverse else self.reach
-        pairs = [(i, i + step) for i in range(self.count) if 0 <= i + step < self.count]
-        self.got = [
-            lax.ppermute(self.cover.astype(BF), "seq", pairs),
-            lax.ppermute(self.fade, "seq", pairs),
-        ]
-
-    def take(self, line):
-        def merge(got, got_fade, cover, fade, border, border_fade):
-            got = got.astype(F32)
-            if border is None:
-                border, border_fade = got, got_fade
-            else:
-                border, border_fade = border + border_fade * got, border_fade * got_fade
-            return border, border_fade, cover + fade * got, fade * got_fade
-
-        border = self.border or (None, None)
-        *self.border, self.cover, self.fade = line(
-            merge, *self.got, self.cover, self.fade, *border
-        )
-        self.reach *= 2
-        if self.reach >= self.count:
-            return True
-        self.send()
-        return False
-
-    def finish(self, line):
-        while not self.take(line):
-            pass
-        return self.border[0]
-
-
-def stream(groups, place, count, weights, outs, body, before=None):
+        count = lax.axis_size("seq")
+        packed = jnp.concatenate([state, jnp.repeat(fade, 16, axis=1)], axis=1).astype(BF)
+        self.got = []
+        for reach in range(1, count):
+            step = -reach if reverse else reach
+            pairs = [(i, i + step) for i in range(count) if 0 <= i + step < count]
+            self.got.append(lax.ppermute(packed, "seq", pairs))
+
+    def take(self, *got):
+        border = None
+        for x in got[::-1]:
+            state, fade = x[:, :HDIM].astype(F32), x[:, HDIM : HDIM + 1].astype(F32)
+            border = state if border is None else state + fade * border
+        return border
+
+
+def stream(groups, first, count, weights, outs, body, before=None):
     chips, rows, width = groups[0][0].shape
     n_sets, n_w, n_out = len(groups), len(weights), len(outs)
-    parts = len(groups[0])
-    n_arrays = parts * n_sets
-    steps = chips if place is None else 1
-    lines = 4 * rows if place is None else chips * 2 * rows
+    n_arrays = 4 * n_sets
 
     def kernel(*refs):
         arrays = refs[:n_arrays]
@@ -248,33 +223,30 @@
         i = pl.program_id(0)
 
         def copies(k):
-            chosen = [(k, part, part) for part in range(4)]
-            if place is not None:
-                chosen = [(c, ab, 2 * c + ab) for c in range(chips) for ab in range(2)]
             return [
                 pltpu.make_async_copy(
-                    arrays[parts * s + part].at[c],
-                    bufs[s].at[k % 2, pl.ds(at * rows, rows)],
-                    sem.at[s, k % 2, at],
+                    arrays[4 * s + part].at[k],
+                    bufs[s].at[k % 2, pl.ds(part * rows, rows)],
+                    sem.at[s, k % 2, part],
                 )
                 for s in range(n_sets)
-                for c, part, at in chosen
+                for part in range(4)
             ]
 
-        for k in range(steps):
+        for k in range(chips):
 
             @pl.when(i == k)
             def _(k=k):
                 if k == 0:
                     for copy in copies(0):
                         copy.start()
-                if k + 1 < steps:
+                if k + 1 < chips:
                     for copy in copies(k + 1):
                         copy.start()
                 for copy in copies(k):
                     copy.wait()
 
-        slot = lax.rem(i, 2) if steps > 1 else 0
+        slot = lax.rem(i, 2)
         results = body([buf[slot] for buf in bufs], w_refs)
         for ref, value in zip(out_refs, results):
             ref[...] = value.reshape(ref.shape).astype(ref.dtype)
@@ -282,25 +254,19 @@
     anywhere = pl.BlockSpec(memory_space=pl.ANY)
     whole = lambda w: pl.BlockSpec(w.shape, lambda i: (0, 0), pipeline_mode=pl.Buffered(1))
     given = [] if before is None else list(before)
-    if place is None:
-        out_spec = lambda c: pl.BlockSpec((1, 2, 2, rows, c), lambda i: (i, 0, 0, 0, 0))
-    else:
-        out_spec = lambda c: pl.BlockSpec((chips, 1, 2, rows, c), lambda i: (1, place, 0, 0, 0))
     return pl.pallas_call(
         kernel,
-        grid=(steps,),
+        grid=(chips,),
         in_specs=[anywhere] * n_arrays + [whole(w) for w in weights] + [anywhere] * len(given),
-        out_specs=[out_spec(c) for c, _ in outs],
-        out_shape=[jax.ShapeDtypeStruct((count // 2, 2, 2, rows, c), d) for c, d in outs],
-        scratch_shapes=[pltpu.VMEM((min(steps, 2), lines, width), BF) for _ in groups]
-        + [pltpu.SemaphoreType.DMA((n_sets, 2, lines // rows))],
+        out_specs=[
+            pl.BlockSpec((2, 2, rows, c), lambda i: (i + first, 0, 0, 0)) for c, _ in outs
+        ],
+        out_shape=[jax.ShapeDtypeStruct((count, 2, rows, c), d) for c, d in outs],
+        scratch_shapes=[pltpu.VMEM((2, 4 * rows, width), BF) for _ in groups]
+        + [pltpu.SemaphoreType.DMA((n_sets, 2, 4))],
         input_output_aliases={n_arrays + n_w + o: o for o in range(len(given))},
         compiler_params=pltpu.CompilerParams(vmem_limit_bytes=VMEM),
     )(*[x for s in groups for x in s], *weights, *given)
-
-
-def by_slot(arrays):
-    return [x.reshape((-1,) + x.shape[2:]) for x in arrays]
 
 
 def head_rows(rows, out_weight, count):
@@ -323,42 +289,82 @@
     )(rows, out_weight)
 
 
+def products(refs, n, dims):
+    total = None
+    for left, weight in zip(refs[:n], refs[n : 2 * n]):
+        value = left[...]
+        part = dot(value.reshape(-1, value.shape[-1]), weight[...], dims)
+        total = part if total is None else total + part
+    return total.astype(BF)
+
+
 def partial_rows(lefts, weights, dims, parity):
     count, _, rows, _ = lefts[0].shape
     width = weights[0].shape[1 if dims == NN else 0]
     n = len(lefts)
 
     def kernel(*refs):
-        total = None
-        for left, weight in zip(refs[:n], refs[n : 2 * n]):
-            value = left[...].reshape(2 * rows, left.shape[-1])
-            part = dot(value, weight[...], dims)
-            total = part if total is None else total + part
-        refs[2 * n][...] = total.astype(BF).reshape(2, 1, rows, width)
+        total = products(refs, n, dims).reshape(2, 2, rows, width)
+        for ab in range(2):
+            refs[2 * n][ab] = total[:, ab]
 
     whole = lambda w: pl.BlockSpec(w.shape, lambda i: (0, 0), pipeline_mode=pl.Buffered(1))
     return pl.pallas_call(
         kernel,
-        grid=(count // 2,),
+        grid=(count // 4,),
         in_specs=[
-            pl.BlockSpec((1, 2, rows, x.shape[-1]), lambda i: (2 * i + parity, 0, 0, 0))
+            pl.BlockSpec((2, 1, 2, rows, x.shape[-1]), lambda i: (i, parity, 0, 0, 0))
             for x in lefts
         ]
         + [whole(w) for w in weights],
-        out_specs=pl.BlockSpec((2, 1, rows, width), lambda i: (0, i, 0, 0)),
+        out_specs=pl.BlockSpec((2, 2, rows, width), lambda i: (0, i, 0, 0)),
         out_shape=jax.ShapeDtypeStruct((2, count // 2, rows, width), BF),
         compiler_params=pltpu.CompilerParams(vmem_limit_bytes=VMEM),
-    )(*lefts, *weights)
-
-
-def owned_rows(left, weight, table):
-    count, _, rows, depth = left.shape
-    width = weight.shape[1]
-
-    def kernel(_, left_ref, weight_ref, a_ref, b_ref):
-        total = dot(left_ref[...].reshape(2 * rows, depth), weight_ref[...], NN).astype(BF)
-        a_ref[...] = total[:rows]
-        b_ref[...] = total[rows:]
+    )(*[x.reshape((count // 2, 2) + x.shape[1:]) for x in lefts], *weights)
+
+
+def owned_rows(lefts, weights, dims, table):
+    count, _, rows, _ = lefts[0].shape
+    width = weights[0].shape[1 if dims == NN else 0]
+    n = len(lefts)
+
+    def kernel(tab, *refs):
+        i = pl.program_id(0)
+        total = products(refs, n, dims).reshape(2, 2, rows, width)
+        for c in range(2):
+            for ab in range(2):
+                refs[2 * n][tab[ab * count + 2 * i + c], ab] = total[c, ab]
+
+    return pl.pallas_call(
+        kernel,
+        grid_spec=pltpu.PrefetchScalarGridSpec(
+            num_scalar_prefetch=1,
+            grid=(count // 2,),
+            in_specs=[
+                pl.BlockSpec((2, 2, rows, x.shape[-1]), lambda i, tab: (i, 0, 0, 0))
+                for x in lefts
+            ]
+            + [
+                pl.BlockSpec(w.shape, lambda i, tab: (0, 0), pipeline_mode=pl.Buffered(1))
+                for w in weights
+            ],
+            out_specs=pl.BlockSpec((count, 2, rows, width), lambda i, tab: (0, 0, 0, 0)),
+        ),
+        out_shape=jax.ShapeDtypeStruct((count, 2, rows, width), BF),
+        compiler_params=pltpu.CompilerParams(vmem_limit_bytes=VMEM),
+    )(table, *lefts, *weights)
+
+
+def outer_rows(moved, rows, table):
+    count, own, cols = moved.shape
+    width = rows.shape[1]
+    half = cols // 2
+
+    def kernel(tab, a_ref, b_ref, rows_ref, out_ref):
+        value = rows_ref[...]
+        for ab, ref in enumerate((a_ref, b_ref)):
+            left = ref[0].astype(F32).T[ab * half : (ab + 1) * half].astype(BF)
+            out_ref[0, ab, 0] = dot(left, value, NN).astype(BF)
 
     return pl.pallas_call(
         kernel,
@@ -366,17 +372,17 @@
             num_scalar_prefetch=1,
             grid=(count,),
             in_specs=[
-                pl.BlockSpec((1, 2, rows, depth), lambda t, tab: (t, 0, 0, 0)),
-                pl.BlockSpec(weight.shape, lambda t, tab: (0, 0), pipeline_mode=pl.Buffered(1)),
+                pl.BlockSpec((1, own, cols), lambda t, tab: (tab[t], 0, 0)),
+                pl.BlockSpec((1, own, cols), lambda t, tab: (tab[count + t], 0, 0)),
+                pl.BlockSpec((own, width), lambda t, tab: (0, 0)),
             ],
-            out_specs=[
-                pl.BlockSpec((rows, width), lambda t, tab: (tab[t], 0)),
-                pl.BlockSpec((rows, width), lambda t, tab: (tab[count + t], 0)),
-            ],
+            out_specs=pl.BlockSpec(
+                (1, 2, 1, half, width), lambda t, tab: (t % 2, 0, t // 2, 0, 0)
+            ),
         ),
-        out_shape=[jax.ShapeDtypeStruct((count * rows, width), BF)] * 2,
+        out_shape=jax.ShapeDtypeStruct((2, 2, count // 2, half, width), BF),
         compiler_params=pltpu.CompilerParams(vmem_limit_bytes=VMEM),
-    )(table, left, weight)
+    )(table, moved, moved, rows)
 
 
 def attend(moved, out_weight, own_rows, gain):
@@ -844,41 +850,40 @@
     joint_weights = (query_weight, forget_weight, input_weight, gate_weight)
     joint_out = [(4 * cols, F32), (width, BF)]
 
-    def project(group, place, before=None):
+    def project(group, first, before=None):
         def body(xs, w_refs):
             return [jnp.concatenate([dot(xs[0], w[...], NN) for w in w_refs], axis=1), xs[0]]
 
         return line(
             lambda group, before: stream(
-                [group], place, count, joint_weights, joint_out, body, before
+                [group], first, count, joint_weights, joint_out, body, before
             ),
             group,
             before,
         )
 
-    part = project(going.early(), None)
+    part = project(going.early(), 0)
     cot_rows = tie(to_rows(cotangent), part[0])
-    other = going.other((part[0], cot_rows))
-    part = project(list(going.late), 0, part)
-    cots = Gather(*tie(halves_of(cot_rows), other))
+    latest = going.latest((part[0], cot_rows))
+    cots = Gather(*tie(halves_of(cot_rows), latest))
     cots.links(False)
-    joint, in_rows = by_slot(project(other, 1, part))
+    joint, in_rows = project(latest, count // 4, part)
     ends, fade, gate_sums = line(scan.ends, joint)
     entry = Entering(ends, fade, False)
     cots.links(True, (ends,))
     mixture, reach, starts, fades = line(scan.forward, joint)
-    initial = entry.finish(line)
+    initial = line(entry.take, *entry.got)
     mixture, gated_p = line(scan.finish, joint, mixture, reach, initial, head_gain)
     moved = lax.all_to_all(
         gated_p.reshape(count, own, cols), "hid", split_axis=0, concat_axis=0, tiled=True
     )
     cot_early = tie((cots.a, cots.b), gated_p)
     cot_early = list(cot_early) + [hop(x, 1) for x in cot_early]
-    cot_other = cots.other((gated_p,))
+    cot_latest = cots.latest((gated_p,))
     residual, normed_feed = line(
         lambda m, _: attend(m, out_weight, own_rows, feed_gain.reshape(1, width)),
         moved,
-        (cot_early, cot_other),
+        (cot_early, cot_latest),
     )
 
     going = Gather(*halves_of(normed_feed))
@@ -887,7 +892,7 @@
     feed_weights = (gate_t, up_t, down_weight)
     feed_shapes = [(units, BF)] * 3 + [(width, BF)] * 2
 
-    def feed(group, cot_group, place, before=None):
+    def feed(group, cot_group, first, before=None):
         def body(xs, w_refs):
             gate = dot(xs[0], w_refs[0][...], NT)
             up = dot(xs[0], w_refs[1][...], NT)
@@ -899,33 +904,34 @@
 
         return line(
             lambda group, cot_group, before: stream(
-                [group, cot_group], place, count, feed_weights, feed_shapes, body, before
+                [group, cot_group], first, count, feed_weights, feed_shapes, body, before
             ),
             group,
             cot_group,
             before,
         )
 
-    part = feed(going.early(), cot_early, None)
-    other = going.other((part[0],))
-    part = feed(list(going.late), list(cots.late), 0, part)
-    hidden, grad_feed_gate, grad_up, feed_rows, grad_rows = by_slot(
-        feed(other, cot_other, 1, part)
+    part = feed(going.early(), cot_early, 0)
+    hidden, grad_feed_gate, grad_up, feed_rows, grad_rows = feed(
+        going.latest((part[0],)), cot_latest, count // 4, part
     )
     hidden_f, gate_f, up_f = flat(hidden), flat(grad_feed_gate), flat(grad_up)
     feed_f, grad_f = flat(feed_rows), flat(grad_rows)
-    sums = Sums()
+    spread = lambda x: lax.psum_scatter(
+        x.reshape(-1, width), "hid", scatter_dimension=0, tiled=True
+    )
+    down_w = line(weight_grad, hidden_f, grad_f)
+    gate_w = line(weight_grad, gate_f, feed_f)
+    up_w = line(weight_grad, up_f, feed_f)
+    down_w, gate_w, up_w = lax.psum((down_w, gate_w, up_w), "seq")
     backs = lambda parity: line(
         lambda *a: partial_rows(a, (gate_t, up_t), NN, parity), grad_feed_gate, grad_up
     )
     shrink = Scatter(backs(1))
     even = backs(0)
-    down_w = sums.push(line(weight_grad, hidden_f, grad_f))
     line(shrink.first, even)
-    gate_w = line(weight_grad, gate_f, feed_f)
     while shrink.more():
-        line(lambda *_: shrink.step())
-    up_w = line(weight_grad, up_f, feed_f)
+        line(lambda: shrink.step())
 
     def after_feed(grad):
         cot = to_rows(cotangent).astype(F32)
@@ -937,39 +943,30 @@
 
     sent = line(lambda rows: head_rows(rows, out_weight, count), grad_attended)
     grad_gated = lax.all_to_all(sent, "hid", split_axis=0, concat_axis=0, tiled=True)
-    sums.tick(line)
-    gate_w = sums.push(gate_w)
-    out_full = line(
-        lambda m, g: lax.dot_general(
-            m, g, (((1,), (0,)), ((), ())), preferred_element_type=F32
-        ).astype(BF),
-        moved,
-        grad_attended,
-    )
+    feed_out = line(lambda *a: owned_rows(a, (down_weight,), NN, offsets), hidden)
+    feed_out = spread(feed_out)
     grad_mix, grad_gate, grad_head, reach = line(
         scan.finish_back, joint, mixture, grad_gated.reshape(mixture.shape), head_gain
     )
-    exit_ = Entering(reach, fade, True)
+    leave = Entering(reach, fade, True)
     in_f = flat(in_rows)
     mix_gate = line(weight_grad, in_f, flat(grad_gate))
-    spread = lambda x: lax.psum_scatter(x, "hid", scatter_dimension=0, tiled=True)
-    out_part = spread(tie(out_full.reshape(count * cols, width), mix_gate))
-    leaving_done = exit_.take(line)
-    feed_a, feed_b = line(owned_rows, hidden, down_weight, offsets)
-    feed_out = jnp.concatenate([spread(feed_a), spread(feed_b)], axis=0)
-    sums.tick(line)
-    up_w = sums.push(up_w)
-    leaving = exit_.border[0] if leaving_done else exit_.finish(line)
+    out_full = line(lambda m, g: outer_rows(m, g, offsets), moved, grad_attended)
+    narrow = Scatter(out_full[1])
+    leaving = line(leave.take, *leave.got)
+    line(narrow.first, out_full[0])
     final = ends + fade * initial
+    sums = Sums()
+    mix_gate = sums.push(tie(mix_gate, leaving))
     grad_three, grad_lower = line(
         scan.backward, joint, grad_mix, starts, fades, initial, final, leaving
     )
-    three_f = flat(grad_three)
+    while narrow.more():
+        line(lambda: narrow.step())
+    three_w = line(weight_grad, in_f, flat(grad_three))
     quarter = width // 4
-    three = lambda i: line(
-        lambda x, g: weight_grad(x[:, i * quarter : (i + 1) * quarter], g), in_f, three_f
-    )
-    threes = [three(0), three(1)]
+    threes = [three_w[i * quarter : (i + 1) * quarter] for i in range(4)]
+    out_part = line(lambda x: x.astype(BF), narrow.result())
     sums.tick(line)
     out_part = sums.push(out_part)
     joint_three = jnp.concatenate(joint_weights[:3], axis=1)
@@ -977,30 +974,30 @@
         lambda *a: partial_rows(a, (joint_three, gate_weight), NT, parity), grad_three, grad_gate
     )
     shrink = Scatter(backs(1))
-    threes += [three(2), three(3)]
+    even = backs(0)
     sums.tick(line)
-    mix_gate = sums.push(mix_gate)
-    even = backs(0)
+    threes[0] = sums.push(threes[0])
     line(shrink.first, even)
     sums.tick(line)
-    threes[0] = sums.push(threes[0])
+    threes[1] = sums.push(threes[1])
     while shrink.more():
-        line(lambda *_: shrink.step())
+        line(lambda: shrink.step())
     sums.tick(line)
-    threes[1] = sums.push(threes[1])
+    threes[2] = sums.push(threes[2])
     grad_in, grad_mixer = line(lambda g: norm_back(inputs, mixer_gain, g, 1e-06), shrink.result())
-    grad_tokens = line(lambda a, b: from_rows(a + b), grad_residual, grad_in)
     small = everywhere(
         jnp.concatenate([grad_mixer, grad_feed_gain, jnp.sum(gate_sums).reshape(1)]), "hid"
     )
+    grad_tokens = line(lambda a, b: from_rows(a + b), grad_residual, grad_in)
     sums.tick(line)
-    threes[2] = sums.push(threes[2])
+    threes[3] = sums.push(threes[3])
     small = everywhere(jnp.concatenate([small, grad_lower[0], grad_head[0]]), "seq")
     heads = small[2 * width + 1 :]
-    sums.tick(line)
-    threes[3] = sums.push(threes[3])
+    down_w, gate_w, up_w = line(
+        lambda d, *x: (d.astype(F32), *[y.astype(F32).T for y in x]), down_w, gate_w, up_w
+    )
+    gathered_out = lax.all_gather(out_part["total"], "hid", axis=0, tiled=True)
     output = line(lambda a, b: from_rows((a + b).astype(BF)), residual, feed_out)
-    gathered_out = lax.all_gather(out_part["total"], "hid", axis=0, tiled=True)
     sums.tick(line)
     grad_out = line(lambda x: x.astype(F32), gathered_out)
     sums.drain(line)
@@ -1019,9 +1016,9 @@
         heads[cols:],
         grad_out,
         small[width : 2 * width],
-        total(gate_w).T,
-        total(up_w).T,
-        total(down_w),
+        gate_w,
+        up_w,
+        down_w,
         mean_forget,
     )
 

time: 975 us -> 894 us (0.917)
  starting transfers between devices: 149 us -> 98.3 us
  matrix products: 61.5 us -> 43.2 us
  local copies, waits for them, and re-layouts: 27.1 us -> 39.4 us
  other arithmetic: 115 us -> 104 us
    ppermute x27 -> x18, starting transfers between devices: 103 us -> 37.8 us  [start(): lax.ppermute(value, 'seq', self.pairs[stage])]
    ppermute x27 -> x18, waiting for transfers between devices: 195 us -> 147 us  [start(): lax.ppermute(value, 'seq', self.pairs[stage])]
    ppermute x6, waiting for transfers between devices: 10.4 us -> 54.8 us  [__init__(): self.got.append(lax.ppermute(packed, 'seq', pairs))]
    convert_element_type x18 -> x12, other arithmetic: 47.8 us -> 18.3 us  [turn(): (a.astype(F32) + b.astype(F32)).astype(BF)]
    dot_general x8 -> x5, matrix products: 55.7 us -> 43.2 us  [weight_grad(): lax.dot_general(left, right, TN, preferred_element_type=F32).astype(BF)]
    ppermute x5, starting transfers between devices: 3.38 us -> 13.3 us  [everywhere(): lax.ppermute(value, axis, [(i, i ^ mask) for i in range(count)])]
    convert_element_type x4 -> x6, other arithmetic: 11.8 us -> 19.7 us  [step(): sum((x[half:].astype(F32) for x in kept)).astype(BF)]
    pallas_call x10 -> x9, Pallas kernels: 112 us -> 106 us  [the longest x4 55.5 us: stream(): pl.pallas_call(kernel, grid=(chips,), in_specs=[anywhere] * n_arrays + [w...]
  transfers between devices with their start and end apart: 77 -> 72, of which waited for: 35 -> 37; matrix products, arithmetic and copies ran while one was open for 18% -> 15% of each run, Pallas kernels for 20% -> 22%
where the time goes in v2:
time: 894 us; the launch traced here: 884 us
  waiting for transfers between devices  327 us (37%)
  Pallas kernels  232 us (26%)
  other arithmetic  104 us (12%)
  starting transfers between devices  98.3 us (11%)
  matrix products  43.2 us (5%)
  local copies, waits for them, and re-layouts  39.4 us (4%)
  blocking collectives  19.8 us (2%)
  between operations  19.5 us (2%)
    ppermute x18, waiting for transfers between devices, start(): lax.ppermute(value, 'seq', self.pairs[stage])  147 us
    ppermute x39, waiting for transfers between devices, hop(): return lax.ppermute(array, 'hid', [(i, i ^ mask) for i in range(count)])  118 us
    pallas_call x5, Pallas kernels, call(): pl.pallas_call(kernel, grid_spec=pltpu.PrefetchScalarGridSpec(num_scalar_...  95.8 us
    pallas_call x4, Pallas kernels, stream(): pl.pallas_call(kernel, grid=(chips,), in_specs=[anywhere] * n_arrays + [w...  55.5 us
    ppermute x6, waiting for transfers between devices, __init__(): self.got.append(lax.ppermute(packed, 'seq', pairs))  54.8 us
    dot_general x5, matrix products, weight_grad(): lax.dot_general(left, right, TN, preferred_element_type=F32).astype(BF)  43.2 us
    pallas_call x4, Pallas kernels, partial_rows(): pl.pallas_call(kernel, grid=(count // 4,), in_specs=[pl.BlockSpec((2, 1,...  40.4 us
    ppermute x18, starting transfers between devices, start(): lax.ppermute(value, 'seq', self.pairs[stage])  37.8 us
  transfers between devices with their start and end apart: 72, of which 37 were waited for; matrix products, arithmetic and copies ran while one was open for 15% of the time, Pallas kernels for 22%

profile of v2, /device:TPU:0, one launch (start us, length us, event | category | flops | bytes accessed | tf_op | source)
XLA Modules:
  0.0 883.7 jit_solution(873233008980482338)
XLA Ops:
  17.2 10.4 %collective-permute-done.2 = bf16[1,128,2048]{2,1,0:T(8,128)(2,1)S(1)} collective-permute-done((bf16[1,128,2048]{2,1,0:T(8,128)(2,1)S(1)}, bf16[1,128,2048]{2,1,0:T(8,128)(2,1)S(1)}, u32[]{:S(2)}, u32[]{:S(2)}) %collective-permute-start.2) | collective-permute-done | bytes 524320 | tf_op jit(solution)/shard_map/ppermute | solution.py:48
  34.2 9.8 %shard_map.280 = (f32[8,2,128,1024]{3,2,1,0:T(8,128)}, bf16[8,2,128,2048]{3,2,1,0:T(8,128)(2,1)}) custom-call(bf16[2,128,2048]{2,1,0:T(8,128)(2,1)} %pad_maximum_fusion.3.refs_0_, bf16[2,128,2048]{2,1,0:T(8,128)(2,1)} %copy-done.20, bf16[2,128,2048]{2,1,0:T(8,128)(2,1)} %collective-permute-done.4.refs_2_, bf16[2,128,2048]{2,1,0:T(8,128)(2,1)} %copy-done.41, ...), custom_call_target="tpu_custom_call" | custom-call | tf_op jit(solution)/shard_map/pallas_call | solution.py:257
  44.0 11.8 %collective-permute-done.3.refs_1_ = bf16[2,128,2048]{2,1,0:T(8,128)(2,1)} collective-permute-done((bf16[2,128,2048]{2,1,0:T(8,128)(2,1)S(1)}, bf16[2,128,2048]{2,1,0:T(8,128)(2,1)}, u32[]{:S(2)}, u32[]{:S(2)}) %collective-permute-start.3) | collective-permute-done | bytes 1048608 | tf_op jit(solution)/shard_map/ppermute | solution.py:48
  65.1 9.8 %shard_map.281 = (f32[8,2,128,1024]{3,2,1,0:T(8,128)}, bf16[8,2,128,2048]{3,2,1,0:T(8,128)(2,1)}) custom-call(bf16[2,128,2048]{2,1,0:T(8,128)(2,1)} %collective-permute-done.1.refs_0_, bf16[2,128,2048]{2,1,0:T(8,128)(2,1)} %collective-permute-done.3.refs_1_, bf16[2,128,2048]{2,1,0:T(8,128)(2,1)} %copy-done.36, ...), custom_call_target="tpu_custom_call", output_to_operand_aliasing={{0}: (8, {}), {1}: (9, {})} | custom-call | tf_op jit(solution)/shard_map/pallas_call | solution.py:257
  74.9 12.0 %shard_map.282 = (f32[8,128,128]{2,1,0:T(8,128)}, f32[8,1,128]{2,1,0:T(1,128)}, f32[1,256]{1,0:T(1,128)}) custom-call(s32[21]{0:T(128)} %pad_add_fusion.sc, f32[8,2,128,1024]{3,2,1,0:T(8,128)} %get-tuple-element.289.fa_ref.fb_ref.va_ref.vb_ref.ja_ref.jb_ref.ga_ref.gb_ref.qa_ref.qb_ref, ...), custom_call_target="tpu_custom_call" | custom-call | tf_op jit(solution)/shard_map/pallas_call | solution.py:468
  103.0 21.0 %shard_map.283 = (f32[8,2,128,256]{3,2,1,0:T(8,128)}, f32[8,2,128,256]{3,2,1,0:T(8,128)}, f32[8,8,128,128]{3,2,1,0:T(8,128)}, f32[8,8,1,128]{3,2,1,0:T(1,128)}) custom-call(s32[21]{0:T(128)} %pad_add_fusion.sc, f32[8,2,128,1024]{3,2,1,0:T(8,128)} %get-tuple-element.289.fa_ref.fb_ref.va_ref.vb_ref.ja_ref.jb_ref.ga_ref.gb_ref.qa_ref.qb_ref, ...), custom_call_target="tpu_custom_call" | custom-call | tf_op jit(solution)/shard_map/pallas_call | solution.py:468
  127.0 10.2 %shard_map.284 = (f32[8,2,128,256]{3,2,1,0:T(8,128)}, bf16[8,2,128,256]{3,2,1,0:T(8,128)(2,1)}) custom-call(s32[21]{0:T(128)} %pad_add_fusion.sc, f32[8,2,128,1024]{3,2,1,0:T(8,128)} %get-tuple-element.289.fa_ref.fb_ref.va_ref.vb_ref.ja_ref.jb_ref.ga_ref.gb_ref.qa_ref.qb_ref, ...), custom_call_target="tpu_custom_call" | custom-call | tf_op jit(solution)/shard_map/pallas_call | solution.py:468
  138.4 19.8 %all_to_all.10.moved_ref.a_ref.b_ref = bf16[8,256,256]{2,1,0:T(8,128)(2,1)} all-to-all(bf16[8,256,256]{2,1,0:T(8,128)(2,1)} %bitcast.220), channel_id=1, replica_groups=mesh['seq'=4,'hid'=8] {'hid'}, dimensions={0} | all-to-all | bytes 2097152 | tf_op jit(solution)/shard_map/all_to_all | solution.py:877
  172.9 11.9 %collective-permute-done.21 = bf16[1,128,2048]{2,1,0:T(8,128)(2,1)S(1)} collective-permute-done((bf16[1,128,2048]{2,1,0:T(8,128)(2,1)S(1)}, bf16[1,128,2048]{2,1,0:T(8,128)(2,1)S(1)}, u32[]{:S(2)}, u32[]{:S(2)}) %collective-permute-start.21) | collective-permute-done | bytes 524320 | tf_op jit(solution)/shard_map/ppermute | solution.py:48
  190.1 17.9 %shard_map.286 = (bf16[8,2,128,704]{3,2,1,0:T(8,128)(2,1)}, bf16[8,2,128,704]{3,2,1,0:T(8,128)(2,1)}, bf16[8,2,128,704]{3,2,1,0:T(8,128)(2,1)}, bf16[8,2,128,204...) custom-call(bf16[2,128,2048]{2,1,0:T(8,128)(2,1)} %copy-done.18, bf16[2,128,2048]{2,1,0:T(8,128)(2,1)} %copy-done.17, ...), custom_call_target="tpu_custom_call" | custom-call | tf_op jit(solution)/shard_map/pallas_call | solution.py:257
  217.3 18.0 %shard_map.287 = (bf16[8,2,128,704]{3,2,1,0:T(8,128)(2,1)}, bf16[8,2,128,704]{3,2,1,0:T(8,128)(2,1)}, bf16[8,2,128,704]{3,2,1,0:T(8,128)(2,1)}, bf16[8,2,128,204...) custom-call(bf16[2,128,2048]{2,1,0:T(8,128)(2,1)} %collective-permut, ...), custom_call_target="tpu_custom_call", output_to_operand_aliasing={{0}: (11, {}), {1}: (12, {}), {2}: (13, {}), {3}: (14, {}),... | custom-call | tf_op jit(solution)/shard_map/pallas_call | solution.py:257
  235.3 11.1 %convolution_convert_fusion.3 = bf16[704,2048]{1,0:T(8,128)(2,1)} fusion(bf16[2048,704]{1,0:T(8,128)(2,1)} %bitcast.199, bf16[2048,2048]{1,0:T(8,128)(2,1)} %bitcast.206), kind=kOutput, calls=%fused_computation.8 | convolution fusion | flops 5907021824 | bytes 14155776 | tf_op jit(solution)/shard_map/dot_general | solution.py:796
  261.8 11.4 %shard_map.288 = bf16[2,4,128,2048]{3,2,1,0:T(8,128)(2,1)} custom-call(bf16[4,2,2,128,704]{4,3,2,1,0:T(8,128)(2,1)} %bitcast.189, bf16[4,2,2,128,704]{4,3,2,1,0:T(8,128)(2,1)} %bitcast.192, bf16[704,2048]{1,0:T(8,128)(2,1)} %bitcast.182, bf16[704,2048]{1,0:T(8,128)(2,1)} %bitcast.186), custom_call_target="tpu_custom_call" | custom-call | tf_op jit(solution)/shard_map/pallas_call | solution.py:312
  273.3 11.8 %shard_map.289 = bf16[2,4,128,2048]{3,2,1,0:T(8,128)(2,1)} custom-call(bf16[4,2,2,128,704]{4,3,2,1,0:T(8,128)(2,1)} %bitcast.190, bf16[4,2,2,128,704]{4,3,2,1,0:T(8,128)(2,1)} %bitcast.193, bf16[704,2048]{1,0:T(8,128)(2,1)} %bitcast.183, bf16[704,2048]{1,0:T(8,128)(2,1)} %bitcast.187), custom_call_target="tpu_custom_call" | custom-call | tf_op jit(solution)/shard_map/pallas_call | solution.py:312
  291.7 23.5 %collective-permute-done.28 = bf16[2,128,2048]{2,1,0:T(8,128)(2,1)} collective-permute-done((bf16[2,128,2048]{2,1,0:T(8,128)(2,1)}, bf16[2,128,2048]{2,1,0:T(8,128)(2,1)}, u32[]{:S(2)}, u32[]{:S(2)}) %collective-permute-start.28) | collective-permute-done | bytes 1048608 | tf_op jit(solution)/shard_map/ppermute | solution.py:48
  320.4 11.6 %collective-permute-done.29 = bf16[1,128,2048]{2,1,0:T(8,128)(2,1)S(1)} collective-permute-done((bf16[1,128,2048]{2,1,0:T(8,128)(2,1)S(1)}, bf16[1,128,2048]{2,1,0:T(8,128)(2,1)S(1)}, u32[]{:S(2)}, u32[]{:S(2)}) %collective-permute-start.29) | collective-permute-done | bytes 524320 | tf_op jit(solution)/shard_map/ppermute | solution.py:48
  351.6 13.6 %shard_map.291 = bf16[8,2,128,2048]{3,2,1,0:T(8,128)(2,1)} custom-call(s32[16]{0:T(128)} %broadcast_xor_fusion.tab, bf16[8,2,128,704]{3,2,1,0:T(8,128)(2,1)} %get-tuple-element.270.refs_0_, bf16[704,2048]{1,0:T(8,128)(2,1)} %refs_1_.1), custom_call_target="tpu_custom_call" | custom-call | tf_op jit(solution)/shard_map/pallas_call | solution.py:338
  367.3 12.8 %shard_map.292 = (f32[8,2,128,256]{3,2,1,0:T(8,128)}, bf16[8,2,128,256]{3,2,1,0:T(8,128)(2,1)}, f32[1,256]{1,0:T(1,128)}, f32[8,128,128]{2,1,0:T(8,128)}) custom-call(s32[21]{0:T(128)} %pad_add_fusion.sc, f32[8,2,128,1024]{3,2,1,0:T(8,128)} %get-tuple-element.289.fa_ref.fb_ref.va_ref.vb_ref.ja_ref.jb_ref.ga_ref.gb_ref.qa_ref.qb_ref, ...), custom_call_target="tpu_custom_call" | custom-call | tf_op jit(solution)/shard_map/pallas_call | solution.py:468
  386.3 9.8 %shard_map.293 = bf16[2,2,4,128,2048]{4,3,2,1,0:T(8,128)(2,1)} custom-call(s32[16]{0:T(128)} %broadcast_xor_fusion.tab, bf16[8,256,256]{2,1,0:T(8,128)(2,1)} %all_to_all.10.moved_ref.a_ref.b_ref, bf16[8,256,256]{2,1,0:T(8,128)(2,1)} %all_to_all.10.moved_ref.a_ref.b_ref, bf16[256,2048]{1,0:T(8,128)(2,1)} %get-tuple-element.284.rows_ref), custom_call_target="tpu_custom_call" | custom-call | tf_op jit(solution)/shard_map/pallas_call | solution.py:369
  406.4 20.2 %collective-permute-done.32 = bf16[8,144,128]{2,1,0:T(8,128)(2,1)} collective-permute-done((bf16[8,144,128]{2,1,0:T(8,128)(2,1)S(1)}, bf16[8,144,128]{2,1,0:T(8,128)(2,1)}, u32[]{:S(2)}, u32[]{:S(2)}) %collective-permute-start.32) | collective-permute-done | bytes 294944 | tf_op jit(solution)/shard_map/ppermute | solution.py:203
  426.6 34.6 %collective-permute-done.33 = bf16[8,144,128]{2,1,0:T(8,128)(2,1)} collective-permute-done((bf16[8,144,128]{2,1,0:T(8,128)(2,1)S(1)}, bf16[8,144,128]{2,1,0:T(8,128)(2,1)}, u32[]{:S(2)}, u32[]{:S(2)}) %collective-permute-start.33) | collective-permute-done | bytes 294944 | tf_op jit(solution)/shard_map/ppermute | solution.py:203
  477.9 39.9 %shard_map.294 = (bf16[8,2,128,768]{3,2,1,0:T(8,128)(2,1)}, f32[1,256]{1,0:T(1,128)}) custom-call(s32[21]{0:T(128)} %pad_add_fusion.sc, f32[8,2,128,1024]{3,2,1,0:T(8,128)} %get-tuple-element.289.fa_ref.fb_ref.va_ref.vb_ref.ja_ref.jb_ref.ga_ref.gb_ref.qa_ref.qb_ref, ...), custom_call_target="tpu_custom_call" | custom-call | tf_op jit(solution)/shard_map/pallas_call | solution.py:468
  521.6 10.5 %convolution_convert_fusion = bf16[2048,768]{1,0:T(8,128)(2,1)} fusion(bf16[2048,2048]{1,0:T(8,128)(2,1)} %bitcast.202, bf16[2048,768]{1,0:T(8,128)(2,1)S(1)} %bitcast.198), kind=kOutput, calls=%fused_computation.5 | convolution fusion | flops 6444023808 | bytes 14680064 | tf_op jit(solution)/shard_map/dot_general | solution.py:796
  564.6 31.4 %collective-permute-done.41 = bf16[256,2048]{1,0:T(8,128)(2,1)} collective-permute-done((bf16[256,2048]{1,0:T(8,128)(2,1)}, bf16[256,2048]{1,0:T(8,128)(2,1)}, u32[]{:S(2)}, u32[]{:S(2)}) %collective-permute-start.41) | collective-permute-done | bytes 1048608 | tf_op jit(solution)/shard_map/ppermute | solution.py:137
  612.6 26.9 %collective-permute-done.42 = bf16[512,768]{1,0:T(8,128)(2,1)S(1)} collective-permute-done((bf16[512,768]{1,0:T(8,128)(2,1)S(1)}, bf16[512,768]{1,0:T(8,128)(2,1)S(1)}, u32[]{:S(2)}, u32[]{:S(2)}) %collective-permute-start.42) | collective-permute-done | bytes 786464 | tf_op jit(solution)/shard_map/ppermute | solution.py:137
  641.0 21.0 %collective-permute-done.59 = bf16[2048,256]{1,0:T(8,128)(2,1)S(1)} collective-permute-done((bf16[2048,256]{1,0:T(8,128)(2,1)S(1)}, bf16[2048,256]{1,0:T(8,128)(2,1)S(1)}, u32[]{:S(2)}, u32[]{:S(2)}) %collective-permute-start.59) | collective-permute-done | bytes 1048608 | tf_op jit(solution)/shard_map/ppermute | solution.py:137
  664.3 29.3 %collective-permute-done.60 = bf16[256,2048]{1,0:T(8,128)(2,1)} collective-permute-done((bf16[256,2048]{1,0:T(8,128)(2,1)S(1)}, bf16[256,2048]{1,0:T(8,128)(2,1)}, u32[]{:S(2)}, u32[]{:S(2)}) %collective-permute-start.60) | collective-permute-done | bytes 1048608 | tf_op jit(solution)/shard_map/ppermute | solution.py:137
  700.4 14.7 %collective-permute-done.43 = bf16[512,768]{1,0:T(8,128)(2,1)} collective-permute-done((bf16[512,768]{1,0:T(8,128)(2,1)}, bf16[512,768]{1,0:T(8,128)(2,1)}, u32[]{:S(2)}, u32[]{:S(2)}) %collective-permute-start.43) | collective-permute-done | bytes 786464 | tf_op jit(solution)/shard_map/ppermute | solution.py:137
  721.2 10.8 %collective-permute-done.47 = bf16[2,128,2048]{2,1,0:T(8,128)(2,1)S(1)} collective-permute-done((bf16[2,128,2048]{2,1,0:T(8,128)(2,1)}, bf16[2,128,2048]{2,1,0:T(8,128)(2,1)S(1)}, u32[]{:S(2)}, u32[]{:S(2)}) %collective-permute-start.47) | collective-permute-done | bytes 1048608 | tf_op jit(solution)/shard_map/ppermute | solution.py:48
  740.5 17.9 %collective-permute-done.51 = bf16[1,128,2048]{2,1,0:T(8,128)(2,1)S(1)} collective-permute-done((bf16[1,128,2048]{2,1,0:T(8,128)(2,1)S(1)}, bf16[1,128,2048]{2,1,0:T(8,128)(2,1)S(1)}, u32[]{:S(2)}, u32[]{:S(2)}) %collective-permute-start.51) | collective-permute-done | bytes 524320 | tf_op jit(solution)/shard_map/ppermute | solution.py:48
  830.4 11.7 %convert_element_type.709 = f32[2048,2048]{1,0:T(8,128)} convert(bf16[2048,2048]{1,0:T(8,128)(2,1)} %all-gather.2.cloned.1.call-done) | non-fusion elementwise | flops 4194304 | bytes 25165824 | tf_op jit(solution)/shard_map/convert_element_type | solution.py:1002
  857.7 13.6 %collective-permute-done.67 = bf16[512,768]{1,0:T(8,128)(2,1)S(1)} collective-permute-done((bf16[512,768]{1,0:T(8,128)(2,1)S(1)}, bf16[512,768]{1,0:T(8,128)(2,1)S(1)}, u32[]{:S(2)}, u32[]{:S(2)}) %collective-permute-start.67) | collective-permute-done | bytes 786464 | tf_op jit(solution)/shard_map/ppermute | solution.py:137
  (355 shorter events, 323.7 us)
Async XLA Ops:
  8.0 800.1 %all-reduce.3.cloned.1.call-start = ((), (), s32[]{:S(2)}) async-start(), calls=%async_computation.5 | async-start | bytes 17301504 | tf_op jit(solution)/shard_map/psum | solution.py:926
  30.1 25.7 %collective-permute-start.3 = (bf16[2,128,2048]{2,1,0:T(8,128)(2,1)S(1)}, bf16[2,128,2048]{2,1,0:T(8,128)(2,1)}, u32[]{:S(2)}, u32[]{:S(2)}) collective-permute-start(bf16[2,128,2048]{2,1,0:T(8,128)(2,1)S(1)} %pad_maximum_fusion.4.refs_1_), channel_id=1, source_target_pairs={{0,2},{1,3},{2,0},{3,1},{4,6},{5,7},{6,4},{7,5},{8,10},{9,11},{10,... | collective-permute-start | bytes 3145736 | tf_op jit(solution)/shard_map/ppermute | solution.py:48
  31.6 25.6 %collective-permute-start.1 = (bf16[2,128,2048]{2,1,0:T(8,128)(2,1)}, bf16[2,128,2048]{2,1,0:T(8,128)(2,1)}, u32[]{:S(2)}, u32[]{:S(2)}) collective-permute-start(bf16[2,128,2048]{2,1,0:T(8,128)(2,1)} %pad_maximum_fusion.3.refs_0_), channel_id=1, source_target_pairs={{0,4},{1,5},{2,6},{3,7},{4,0},{5,1},{6,2},{7,3},{8,12},{9,13},{10,... | collective-permute-start | bytes 3145736 | tf_op jit(solution)/shard_map/ppermute | solution.py:48
  89.7 48.1 %collective-permute-start.15 = (bf16[2,128,2048]{2,1,0:T(8,128)(2,1)S(1)}, bf16[2,128,2048]{2,1,0:T(8,128)(2,1)}, u32[]{:S(2)}, u32[]{:S(2)}) collective-permute-start(bf16[2,128,2048]{2,1,0:T(8,128)(2,1)S(1)} %pad_maximum_fusion.5.refs_4_), channel_id=1, source_target_pairs={{0,4},{1,5},{2,6},{3,7},{4,0},{5,1},{6,2},{7,3},{8,12},{9,13},{10,... | collective-permute-start | bytes 3145736 | tf_op jit(solution)/shard_map/ppermute | solution.py:48
  91.2 46.7 %collective-permute-start.16 = (bf16[2,128,2048]{2,1,0:T(8,128)(2,1)S(1)}, bf16[2,128,2048]{2,1,0:T(8,128)(2,1)}, u32[]{:S(2)}, u32[]{:S(2)}) collective-permute-start(bf16[2,128,2048]{2,1,0:T(8,128)(2,1)S(1)} %pad_maximum_fusion.6.refs_5_), channel_id=1, source_target_pairs={{0,2},{1,3},{2,0},{3,1},{4,6},{5,7},{6,4},{7,5},{8,10},{9,11},{10,... | collective-permute-start | bytes 3145736 | tf_op jit(solution)/shard_map/ppermute | solution.py:48
  92.8 31.2 %collective-permute-start.10 = (bf16[8,144,128]{2,1,0:T(8,128)(2,1)S(1)}, bf16[8,144,128]{2,1,0:T(8,128)(2,1)}, u32[]{:S(2)}, u32[]{:S(2)}) collective-permute-start(bf16[8,144,128]{2,1,0:T(8,128)(2,1)S(1)} %pad_maximum_fusion.10), channel_id=1, source_target_pairs={{0,24},{1,25},{2,26},{3,27},{4,28},{5,29},{6,30},{7,31}} | collective-permute-start | bytes 884744 | tf_op jit(solution)/shard_map/ppermute | solution.py:203
  99.0 25.0 %collective-permute-start.8 = (bf16[8,144,128]{2,1,0:T(8,128)(2,1)S(1)}, bf16[8,144,128]{2,1,0:T(8,128)(2,1)}, u32[]{:S(2)}, u32[]{:S(2)}) collective-permute-start(bf16[8,144,128]{2,1,0:T(8,128)(2,1)S(1)} %pad_maximum_fusion.10), channel_id=1, source_target_pairs={{0,8},{8,16},{16,24},{1,9},{9,17},{17,25},{2,10},{10,18},{18,26},{... | collective-permute-start | bytes 884744 | tf_op jit(solution)/shard_map/ppermute | solution.py:203
  185.7 25.3 %collective-permute-start.22 = (bf16[2,128,2048]{2,1,0:T(8,128)(2,1)S(1)}, bf16[2,128,2048]{2,1,0:T(8,128)(2,1)}, u32[]{:S(2)}, u32[]{:S(2)}) collective-permute-start(bf16[2,128,2048]{2,1,0:T(8,128)(2,1)S(1)} %pad_maximum_fusion.8.refs_1_), channel_id=1, source_target_pairs={{0,2},{1,3},{2,0},{3,1},{4,6},{5,7},{6,4},{7,5},{8,10},{9,11},{10,... | collective-permute-start | bytes 3145736 | tf_op jit(solution)/shard_map/ppermute | solution.py:48
  289.5 25.8 %collective-permute-start.28 = (bf16[2,128,2048]{2,1,0:T(8,128)(2,1)}, bf16[2,128,2048]{2,1,0:T(8,128)(2,1)}, u32[]{:S(2)}, u32[]{:S(2)}) collective-permute-start(bf16[2,128,2048]{2,1,0:T(8,128)(2,1)} %get-tuple-element.386), channel_id=1, source_target_pairs={{0,4},{1,5},{2,6},{3,7},{4,0},{5,1},{6,2},{7,3},{8,12},{9,13},{10,... | collective-permute-start | bytes 3145736 | tf_op jit(solution)/shard_map/ppermute | solution.py:48
  291.0 25.5 %collective-permute-start.30 = (bf16[2,128,2048]{2,1,0:T(8,128)(2,1)}, bf16[2,128,2048]{2,1,0:T(8,128)(2,1)}, u32[]{:S(2)}, u32[]{:S(2)}) collective-permute-start(bf16[2,128,2048]{2,1,0:T(8,128)(2,1)} %get-tuple-element.387), channel_id=1, source_target_pairs={{0,2},{1,3},{2,0},{3,1},{4,6},{5,7},{6,4},{7,5},{8,10},{9,11},{10,... | collective-permute-start | bytes 3145736 | tf_op jit(solution)/shard_map/ppermute | solution.py:48
  351.0 462.3 %reduce-scatter.2.cloned.1.call-start = ((), (), s32[]{:S(2)}) async-start(), calls=%async_computation.3 | async-start | bytes 9437184 | tf_op jit(solution)/shard_map/reduce_scatter | solution.py:920
  402.3 62.4 %collective-permute-start.35 = (bf16[2,4,128,2048]{3,2,1,0:T(8,128)(2,1)}, bf16[2,4,128,2048]{3,2,1,0:T(8,128)(2,1)}, u32[]{:S(2)}, u32[]{:S(2)}) collective-permute-start(bf16[2,4,128,2048]{3,2,1,0:T(8,128)(2,1)} %get-tuple-element.381), channel_id=1, source_target_pairs={{0,1},{1,0},{2,3},{3,2},{4,5},{5,4},{6,7},{7,6},{8,9},{9,8},{10,11... | collective-permute-start | bytes 12582920 | tf_op jit(solution)/shard_map/ppermute | solution.py:48
  403.7 57.5 %collective-permute-start.33 = (bf16[8,144,128]{2,1,0:T(8,128)(2,1)S(1)}, bf16[8,144,128]{2,1,0:T(8,128)(2,1)}, u32[]{:S(2)}, u32[]{:S(2)}) collective-permute-start(bf16[8,144,128]{2,1,0:T(8,128)(2,1)S(1)} %pad_maximum_fusion.9), channel_id=1, source_target_pairs={{16,0},{24,8},{17,1},{25,9},{18,2},{26,10},{19,3},{27,11},{20,4},{... | collective-permute-start | bytes 884744 | tf_op jit(solution)/shard_map/ppermute | solution.py:203
  405.0 56.2 %collective-permute-start.34 = (bf16[8,144,128]{2,1,0:T(8,128)(2,1)S(1)}, bf16[8,144,128]{2,1,0:T(8,128)(2,1)}, u32[]{:S(2)}, u32[]{:S(2)}) collective-permute-start(bf16[8,144,128]{2,1,0:T(8,128)(2,1)S(1)} %pad_maximum_fusion.9), channel_id=1, source_target_pairs={{24,0},{25,1},{26,2},{27,3},{28,4},{29,5},{30,6},{31,7}} | collective-permute-start | bytes 884744 | tf_op jit(solution)/shard_map/ppermute | solution.py:203
  406.4 424.0 %all-gather.2.cloned.1.call-start = ((), (), s32[]{:S(2)}) async-start(), calls=%async_computation.4 | async-start | bytes 9437184 | tf_op jit(solution)/shard_map/all_gather | solution.py:999
  469.3 48.5 %collective-permute-start.36 = (bf16[2,128,2048]{2,1,0:T(8,128)(2,1)}, bf16[2,128,2048]{2,1,0:T(8,128)(2,1)}, u32[]{:S(2)}, u32[]{:S(2)}) collective-permute-start(bf16[2,128,2048]{2,1,0:T(8,128)(2,1)} %get-tuple-element.379), channel_id=1, source_target_pairs={{0,4},{1,5},{2,6},{3,7},{4,0},{5,1},{6,2},{7,3},{8,12},{9,13},{10,... | collective-permute-start | bytes 3145736 | tf_op jit(solution)/shard_map/ppermute | solution.py:48
  470.6 47.2 %collective-permute-start.38 = (bf16[2,128,2048]{2,1,0:T(8,128)(2,1)}, bf16[2,128,2048]{2,1,0:T(8,128)(2,1)}, u32[]{:S(2)}, u32[]{:S(2)}) collective-permute-start(bf16[2,128,2048]{2,1,0:T(8,128)(2,1)} %get-tuple-element.378), channel_id=1, source_target_pairs={{0,2},{1,3},{2,0},{3,1},{4,6},{5,7},{6,4},{7,5},{8,10},{9,11},{10,... | collective-permute-start | bytes 3145736 | tf_op jit(solution)/shard_map/ppermute | solution.py:48
  475.4 62.3 %collective-permute-start.40 = (bf16[2048,256]{1,0:T(8,128)(2,1)S(1)}, bf16[2048,256]{1,0:T(8,128)(2,1)}, u32[]{:S(2)}, u32[]{:S(2)}) collective-permute-start(bf16[2048,256]{1,0:T(8,128)(2,1)S(1)} %convolution_convert_fusion.4), channel_id=1, source_target_pairs={{0,8},{24,16},{1,9},{25,17},{2,10},{26,18},{3,11},{27,19},{4,12},{... | collective-permute-start | bytes 3145736 | tf_op jit(solution)/shard_map/ppermute | solution.py:137
  548.5 60.4 %collective-permute-start.46 = (bf16[2,4,128,2048]{3,2,1,0:T(8,128)(2,1)}, bf16[2,4,128,2048]{3,2,1,0:T(8,128)(2,1)}, u32[]{:S(2)}, u32[]{:S(2)}) collective-permute-start(bf16[2,4,128,2048]{3,2,1,0:T(8,128)(2,1)} %shard_map.295), channel_id=1, source_target_pairs={{0,1},{1,0},{2,3},{3,2},{4,5},{5,4},{6,7},{7,6},{8,9},{9,8},{10,11... | collective-permute-start | bytes 12582920 | tf_op jit(solution)/shard_map/ppermute | solution.py:48
  548.5 47.5 %collective-permute-start.41 = (bf16[256,2048]{1,0:T(8,128)(2,1)}, bf16[256,2048]{1,0:T(8,128)(2,1)}, u32[]{:S(2)}, u32[]{:S(2)}) collective-permute-start(bf16[256,2048]{1,0:T(8,128)(2,1)} %pad_maximum_fusion.1), channel_id=1, source_target_pairs={{0,8},{24,16},{1,9},{25,17},{2,10},{26,18},{3,11},{27,19},{4,12},{... | collective-permute-start | bytes 3145736 | tf_op jit(solution)/shard_map/ppermute | solution.py:137
  550.9 47.3 %collective-permute-start.44 = (bf16[2048,256]{1,0:T(8,128)(2,1)S(1)}, bf16[2048,256]{1,0:T(8,128)(2,1)}, u32[]{:S(2)}, u32[]{:S(2)}) collective-permute-start(bf16[2048,256]{1,0:T(8,128)(2,1)S(1)} %add_convert_fusion.6), channel_id=1, source_target_pairs={{8,16},{16,8},{9,17},{17,9},{10,18},{18,10},{11,19},{19,11},{12,20... | collective-permute-start | bytes 3145736 | tf_op jit(solution)/shard_map/ppermute | solution.py:137
  598.2 41.3 %collective-permute-start.42 = (bf16[512,768]{1,0:T(8,128)(2,1)S(1)}, bf16[512,768]{1,0:T(8,128)(2,1)S(1)}, u32[]{:S(2)}, u32[]{:S(2)}) collective-permute-start(bf16[512,768]{1,0:T(8,128)(2,1)S(1)} %get-tuple-element.316), channel_id=1, source_target_pairs={{0,8},{24,16},{1,9},{25,17},{2,10},{26,18},{3,11},{27,19},{4,12},{... | collective-permute-start | bytes 2359304 | tf_op jit(solution)/shard_map/ppermute | solution.py:137
  605.4 35.3 %collective-permute-start.45 = (bf16[256,2048]{1,0:T(8,128)(2,1)S(1)}, bf16[256,2048]{1,0:T(8,128)(2,1)S(1)}, u32[]{:S(2)}, u32[]{:S(2)}) collective-permute-start(bf16[256,2048]{1,0:T(8,128)(2,1)S(1)} %add_convert_fusion.5), channel_id=1, source_target_pairs={{8,16},{16,8},{9,17},{17,9},{10,18},{18,10},{11,19},{19,11},{12,20... | collective-permute-start | bytes 3145736 | tf_op jit(solution)/shard_map/ppermute | solution.py:137
  607.6 54.4 %collective-permute-start.59 = (bf16[2048,256]{1,0:T(8,128)(2,1)S(1)}, bf16[2048,256]{1,0:T(8,128)(2,1)S(1)}, u32[]{:S(2)}, u32[]{:S(2)}) collective-permute-start(bf16[2048,256]{1,0:T(8,128)(2,1)S(1)} %add_convert_fusion.4), channel_id=1, source_target_pairs={{8,0},{16,24},{9,1},{17,25},{10,2},{18,26},{11,3},{19,27},{12,4},{... | collective-permute-start | bytes 3145736 | tf_op jit(solution)/shard_map/ppermute | solution.py:137
  663.0 30.6 %collective-permute-start.60 = (bf16[256,2048]{1,0:T(8,128)(2,1)S(1)}, bf16[256,2048]{1,0:T(8,128)(2,1)}, u32[]{:S(2)}, u32[]{:S(2)}) collective-permute-start(bf16[256,2048]{1,0:T(8,128)(2,1)S(1)} %add_convert_fusion.2), channel_id=1, source_target_pairs={{8,0},{16,24},{9,1},{17,25},{10,2},{18,26},{11,3},{19,27},{12,4},{... | collective-permute-start | bytes 3145736 | tf_op jit(solution)/shard_map/ppermute | solution.py:137
  695.8 36.2 %collective-permute-start.47 = (bf16[2,128,2048]{2,1,0:T(8,128)(2,1)}, bf16[2,128,2048]{2,1,0:T(8,128)(2,1)S(1)}, u32[]{:S(2)}, u32[]{:S(2)}) collective-permute-start(bf16[2,128,2048]{2,1,0:T(8,128)(2,1)} %get-tuple-element.373), channel_id=1, source_target_pairs={{0,4},{1,5},{2,6},{3,7},{4,0},{5,1},{6,2},{7,3},{8,12},{9,13},{10,... | collective-permute-start | bytes 3145736 | tf_op jit(solution)/shard_map/ppermute | solution.py:48
  695.9 36.3 %collective-permute-start.52 = (bf16[2,128,2048]{2,1,0:T(8,128)(2,1)}, bf16[2,128,2048]{2,1,0:T(8,128)(2,1)}, u32[]{:S(2)}, u32[]{:S(2)}) collective-permute-start(bf16[2,128,2048]{2,1,0:T(8,128)(2,1)} %get-tuple-element.372), channel_id=1, source_target_pairs={{0,2},{1,3},{2,0},{3,1},{4,6},{5,7},{6,4},{7,5},{8,10},{9,11},{10,... | collective-permute-start | bytes 3145736 | tf_op jit(solution)/shard_map/ppermute | solution.py:48
  715.1 55.5 %collective-permute-start.50 = (bf16[512,768]{1,0:T(8,128)(2,1)}, bf16[512,768]{1,0:T(8,128)(2,1)}, u32[]{:S(2)}, u32[]{:S(2)}) collective-permute-start(bf16[512,768]{1,0:T(8,128)(2,1)} %get-tuple-element.330), channel_id=1, source_target_pairs={{0,8},{24,16},{1,9},{25,17},{2,10},{26,18},{3,11},{27,19},{4,12},{... | collective-permute-start | bytes 2359304 | tf_op jit(solution)/shard_map/ppermute | solution.py:137
  770.6 46.0 %collective-permute-start.64 = (bf16[512,768]{1,0:T(8,128)(2,1)}, bf16[512,768]{1,0:T(8,128)(2,1)}, u32[]{:S(2)}, u32[]{:S(2)}) collective-permute-start(bf16[512,768]{1,0:T(8,128)(2,1)} %get-tuple-element.345), channel_id=1, source_target_pairs={{0,8},{24,16},{1,9},{25,17},{2,10},{26,18},{3,11},{27,19},{4,12},{... | collective-permute-start | bytes 2359304 | tf_op jit(solution)/shard_map/ppermute | solution.py:137
  772.8 32.1 %collective-permute-start.61 = (bf16[512,768]{1,0:T(8,128)(2,1)}, bf16[512,768]{1,0:T(8,128)(2,1)}, u32[]{:S(2)}, u32[]{:S(2)}) collective-permute-start(bf16[512,768]{1,0:T(8,128)(2,1)} %add_convert_fusion.16), channel_id=1, source_target_pairs={{8,0},{16,24},{9,1},{17,25},{10,2},{18,26},{11,3},{19,27},{12,4},{... | collective-permute-start | bytes 2359304 | tf_op jit(solution)/shard_map/ppermute | solution.py:137
  774.1 29.3 %collective-permute-start.49 = (bf16[512,768]{1,0:T(8,128)(2,1)}, bf16[512,768]{1,0:T(8,128)(2,1)}, u32[]{:S(2)}, u32[]{:S(2)}) collective-permute-start(bf16[512,768]{1,0:T(8,128)(2,1)} %add_convert_fusion.17), channel_id=1, source_target_pairs={{8,16},{16,8},{9,17},{17,9},{10,18},{18,10},{11,19},{19,11},{12,20... | collective-permute-start | bytes 2359304 | tf_op jit(solution)/shard_map/ppermute | solution.py:137
  825.8 26.9 %collective-permute-start.65 = (bf16[512,768]{1,0:T(8,128)(2,1)S(1)}, bf16[512,768]{1,0:T(8,128)(2,1)}, u32[]{:S(2)}, u32[]{:S(2)}) collective-permute-start(bf16[512,768]{1,0:T(8,128)(2,1)S(1)} %add_convert_fusion.12), channel_id=1, source_target_pairs={{8,0},{16,24},{9,1},{17,25},{10,2},{18,26},{11,3},{19,27},{12,4},{... | collective-permute-start | bytes 2359304 | tf_op jit(solution)/shard_map/ppermute | solution.py:137
  (99 other events, 1130.6 us)
Sparse Core Ops, SparseCore 0:
  291.8 381.4 all-reduce.2
Sparse Core Ops, SparseCore 1:
  406.4 100.3 reduce-scatter.1
  695.9 75.7 all-gather.1
